TPU v7x, 32 devices: a whole 2x2x4 slice. The times are simulated.
32 devices in a mesh: dp: 4 (over y, x), fsdp: 8 (over z, core).
Axes of the slice: x: 2, y: 2, z: 4, core: 2. Of those that a mesh axis runs over, the one named last changes fastest.
Arguments:
- tokens: bfloat16 [32, 416, 1024], P(('dp', 'fsdp')), may hold values from -6 to 6
- heads_weight: bfloat16 [1024, 3072], P(('dp', 'fsdp')), may hold values from -0.1875 to 0.1875
- merge_weight: bfloat16 [1024, 1024], P(('dp', 'fsdp')), may hold values from -1.5 to 1.5
- up_weight: bfloat16 [1024, 4096], P(('dp', 'fsdp')), may hold values from -0.1875 to 0.1875
- up_bias: bfloat16 [4096], P(('dp', 'fsdp')), may hold values from -3 to 3
- down_weight: bfloat16 [4096, 1024], P(('dp', 'fsdp')), may hold values from -0.09375 to 0.09375
- down_bias: bfloat16 [1024], P(('dp', 'fsdp')), may hold values from -3 to 3
- norm_gain: bfloat16 [1024], P(('dp', 'fsdp')), may hold values from 0.099609375 to 1.8984375
- norm_bias: bfloat16 [1024], P(('dp', 'fsdp')), may hold values from -3 to 3
- offsets: int32 [32], P(('dp', 'fsdp')), may hold values from 1 to 103
- terminal: int32 [32], P(('dp', 'fsdp')), may hold values from 208 to 415, as said below
- cotangent: bfloat16 [32, 416, 1024], P(('dp', 'fsdp')), may hold values from -6 to 6
Outputs:
- block_output: bfloat16 [32, 416, 1024], P(('dp', 'fsdp'))
- grad_tokens: bfloat16 [32, 416, 1024], P(('dp', 'fsdp'))
- grad_heads: float32 [1024, 3072], P(('dp', 'fsdp'))
- grad_merge: float32 [1024, 1024], P(('dp', 'fsdp'))
- grad_up: float32 [1024, 4096], P(('dp', 'fsdp'))
- grad_up_bias: float32 [4096], P(('dp', 'fsdp'))
- grad_down: float32 [4096, 1024], P(('dp', 'fsdp'))
- grad_down_bias: float32 [1024], P(('dp', 'fsdp'))
- grad_gain: float32 [1024], P(('dp', 'fsdp'))
- grad_bias: float32 [1024], P(('dp', 'fsdp'))
Inputs may be any that keep to these rules, and one draw needn't show every extreme that they name: Window w holds a protein from offsets[w] to terminal[w]; positions after terminal[w] are padding.
All inputs are finite; a program needn't handle non-finite values.
Results may differ from a plain program's by a relative error of at most 0.011.
Values may be sent and summed in bfloat16 or wider, within the bound.
No kernel may reach another device: no remote copies, remote signals or barrier semaphores. Data moves between devices by JAX's collectives and lax.ppermute only.
A program may use at most 256 MiB of HBM per device.

v0:
```python
import jax
import jax.numpy as jnp
from jax import lax
from jax.sharding import PartitionSpec as P

HEADS = 16
ROT = 32


eps = 1e-05
big_negative = -1e30
gelu_scale = 0.7978845608028654
gelu_cubic = 0.044715


def angles(length, rotary):
    position = jnp.arange(length, dtype=jnp.float32)
    exponent = jnp.arange(0, rotary, 2, dtype=jnp.float32) / rotary
    phase = position[:, None] * (1.0 / 10000.0**exponent)[None, :]
    return (jnp.cos(phase)[:, None, :], jnp.sin(phase)[:, None, :])


def turn_pairs(values, cosine_table, sine_table, rotary, direction):
    paired = values[..., :rotary].reshape(values.shape[:-1] + (rotary // 2, 2))
    first_half = paired[..., 0]
    second_half = paired[..., 1]
    signed_sine = direction * sine_table
    new_first = first_half * cosine_table - second_half * signed_sine
    new_second = second_half * cosine_table + first_half * signed_sine
    turned = jnp.stack([new_first, new_second], axis=-1).reshape(values.shape[:-1] + (rotary,))
    return jnp.concatenate([turned, values[..., rotary:]], axis=-1)


def allowed_keys(offsets, terminal, length):
    position = jnp.arange(length, dtype=jnp.int32)
    segment = (position[None, :] >= offsets[:, None]).astype(jnp.int32) + (
        position[None, :] > terminal[:, None]
    ).astype(jnp.int32)
    same_segment = segment[:, :, None] == segment[:, None, :]
    causal = position[:, None] >= position[None, :]
    return (same_segment & causal[None])[:, None, :, :]


def gelu_tanh(values):
    inner = gelu_scale * (values + gelu_cubic * values * values * values)
    return 0.5 * values * (1.0 + jnp.tanh(inner))


def gelu_slope(values):
    tanh_value = jnp.tanh(gelu_scale * (values + gelu_cubic * values * values * values))
    return 0.5 * (1.0 + tanh_value) + 0.5 * values * (
        1.0 - tanh_value * tanh_value
    ) * gelu_scale * (1.0 + 3.0 * gelu_cubic * values * values)


def fetch_weights(
    heads_weight, merge_weight, up_weight, up_bias, down_weight, down_bias, norm_gain, norm_bias
):
    return (
        lax.all_gather(heads_weight, ("dp", "fsdp"), axis=0, tiled=True),
        lax.all_gather(merge_weight, ("dp", "fsdp"), axis=0, tiled=True),
        lax.all_gather(up_weight, ("dp", "fsdp"), axis=0, tiled=True),
        lax.all_gather(up_bias, ("dp", "fsdp"), axis=0, tiled=True),
        lax.all_gather(down_weight, ("dp", "fsdp"), axis=0, tiled=True),
        lax.all_gather(down_bias, ("dp", "fsdp"), axis=0, tiled=True),
        lax.all_gather(norm_gain, ("dp", "fsdp"), axis=0, tiled=True),
        lax.all_gather(norm_bias, ("dp", "fsdp"), axis=0, tiled=True),
    )


def reduce_grads(
    grad_heads, grad_merge, grad_up, grad_up_bias, grad_down, grad_down_bias, grad_gain, grad_bias
):
    return (
        lax.psum_scatter(grad_heads, ("dp", "fsdp"), scatter_dimension=0, tiled=True),
        lax.psum_scatter(grad_merge, ("dp", "fsdp"), scatter_dimension=0, tiled=True),
        lax.psum_scatter(grad_up, ("dp", "fsdp"), scatter_dimension=0, tiled=True),
        lax.psum_scatter(grad_up_bias, ("dp", "fsdp"), scatter_dimension=0, tiled=True),
        lax.psum_scatter(grad_down, ("dp", "fsdp"), scatter_dimension=0, tiled=True),
        lax.psum_scatter(grad_down_bias, ("dp", "fsdp"), scatter_dimension=0, tiled=True),
        lax.psum_scatter(grad_gain, ("dp", "fsdp"), scatter_dimension=0, tiled=True),
        lax.psum_scatter(grad_bias, ("dp", "fsdp"), scatter_dimension=0, tiled=True),
    )


def shards(
    tokens,
    heads_weight,
    merge_weight,
    up_weight,
    up_bias,
    down_weight,
    down_bias,
    norm_gain,
    norm_bias,
    offsets,
    terminal,
    cotangent,
):
    heads_full, merge_full, up_full, up_shift, down_full, down_shift, gain_full, shift_full = (
        fetch_weights(
            heads_weight,
            merge_weight,
            up_weight,
            up_bias,
            down_weight,
            down_bias,
            norm_gain,
            norm_bias,
        )
    )
    windows, length, width = tokens.shape
    head_size = width // HEADS
    scale = head_size ** (-0.5)
    residual = tokens.astype(jnp.float32)
    mean_value = jnp.mean(residual, axis=-1, keepdims=True)
    centered = residual - mean_value
    inverse_std = lax.rsqrt(jnp.mean(centered * centered, axis=-1, keepdims=True) + eps)
    normed = centered * inverse_std
    acts = (normed * gain_full.astype(jnp.float32) + shift_full.astype(jnp.float32)).astype(
        jnp.bfloat16
    )
    mixed = jnp.einsum("wld,de->wle", acts, heads_full, preferred_element_type=jnp.float32)
    split_shape = (windows, length, HEADS, head_size)
    cosine_table, sine_table = angles(length, ROT)
    query = (
        turn_pairs(mixed[..., :width].reshape(split_shape), cosine_table, sine_table, ROT, 1.0)
        * scale
    ).astype(jnp.bfloat16)
    keys = turn_pairs(
        mixed[..., width : 2 * width].reshape(split_shape), cosine_table, sine_table, ROT, 1.0
    ).astype(jnp.bfloat16)
    values = mixed[..., 2 * width :].reshape(split_shape).astype(jnp.bfloat16)
    allowed = allowed_keys(offsets, terminal, length)
    scores = jnp.where(
        allowed,
        jnp.einsum("wqhe,wkhe->whqk", query, keys, preferred_element_type=jnp.float32),
        big_negative,
    )
    maxes = jnp.max(scores, axis=-1, keepdims=True)
    expo = jnp.exp(scores - maxes)
    total = jnp.sum(expo, axis=-1, keepdims=True)
    log_total = maxes + jnp.log(total)
    attended = jnp.einsum(
        "whqk,wkhe->wqhe",
        (expo / total).astype(jnp.bfloat16),
        values,
        preferred_element_type=jnp.float32,
    )
    attended = attended.reshape(windows, length, width).astype(jnp.bfloat16)
    attn_out = jnp.einsum("wld,de->wle", attended, merge_full, preferred_element_type=jnp.float32)
    hidden = jnp.einsum(
        "wld,df->wlf", acts, up_full, preferred_element_type=jnp.float32
    ) + up_shift.astype(jnp.float32)
    activated = gelu_tanh(hidden).astype(jnp.bfloat16)
    mlp_out = jnp.einsum(
        "wlf,fd->wld", activated, down_full, preferred_element_type=jnp.float32
    ) + down_shift.astype(jnp.float32)
    block_output = (residual + attn_out + mlp_out).astype(jnp.bfloat16)
    heads_full, merge_full, up_full, up_shift, down_full, down_shift, gain_full, shift_full = (
        fetch_weights(
            heads_weight,
            merge_weight,
            up_weight,
            up_bias,
            down_weight,
            down_bias,
            norm_gain,
            norm_bias,
        )
    )
    grad_down = jnp.einsum("wlf,wld->fd", activated, cotangent, preferred_element_type=jnp.float32)
    grad_down_bias = jnp.sum(cotangent.astype(jnp.float32), axis=(0, 1))
    grad_merge = jnp.einsum("wld,wle->de", attended, cotangent, preferred_element_type=jnp.float32)
    hidden_grad = (
        jnp.einsum("wld,fd->wlf", cotangent, down_full, preferred_element_type=jnp.float32)
        * gelu_slope(hidden)
    ).astype(jnp.bfloat16)
    grad_up = jnp.einsum("wld,wlf->df", acts, hidden_grad, preferred_element_type=jnp.float32)
    grad_up_bias = jnp.sum(hidden_grad.astype(jnp.float32), axis=(0, 1))
    acts_grad = jnp.einsum("wlf,df->wld", hidden_grad, up_full, preferred_element_type=jnp.float32)
    attended_grad = (
        jnp.einsum("wle,de->wld", cotangent, merge_full, preferred_element_type=jnp.float32)
        .astype(jnp.bfloat16)
        .reshape(split_shape)
    )
    scores = jnp.where(
        allowed,
        jnp.einsum("wqhe,wkhe->whqk", query, keys, preferred_element_type=jnp.float32),
        big_negative,
    )
    probs = jnp.exp(scores - log_total)
    probs_grad = jnp.einsum(
        "wqhe,wkhe->whqk", attended_grad, values, preferred_element_type=jnp.float32
    )
    values_grad = jnp.einsum(
        "whqk,wqhe->wkhe",
        probs.astype(jnp.bfloat16),
        attended_grad,
        preferred_element_type=jnp.float32,
    )
    weighted = jnp.sum(probs * probs_grad, axis=-1, keepdims=True)
    scores_grad = (probs * (probs_grad - weighted)).astype(jnp.bfloat16)
    query_grad = (
        jnp.einsum("whqk,wkhe->wqhe", scores_grad, keys, preferred_element_type=jnp.float32) * scale
    )
    keys_grad = jnp.einsum(
        "whqk,wqhe->wkhe", scores_grad, query, preferred_element_type=jnp.float32
    )
    query_grad = turn_pairs(query_grad, cosine_table, sine_table, ROT, -1.0)
    keys_grad = turn_pairs(keys_grad, cosine_table, sine_table, ROT, -1.0)
    mixed_grad = jnp.concatenate(
        [
            query_grad.reshape(windows, length, width),
            keys_grad.reshape(windows, length, width),
            values_grad.reshape(windows, length, width),
        ],
        axis=-1,
    ).astype(jnp.bfloat16)
    grad_heads = jnp.einsum("wld,wle->de", acts, mixed_grad, preferred_element_type=jnp.float32)
    acts_grad = acts_grad + jnp.einsum(
        "wle,de->wld", mixed_grad, heads_full, preferred_element_type=jnp.float32
    )
    grad_gain = jnp.sum(acts_grad * normed, axis=(0, 1))
    grad_bias = jnp.sum(acts_grad, axis=(0, 1))
    normed_grad = acts_grad * gain_full.astype(jnp.float32)
    input_term = inverse_std * (
        normed_grad
        - jnp.mean(normed_grad, axis=-1, keepdims=True)
        - normed * jnp.mean(normed_grad * normed, axis=-1, keepdims=True)
    )
    grad_tokens = (cotangent.astype(jnp.float32) + input_term).astype(jnp.bfloat16)
    summed = reduce_grads(
        grad_heads,
        grad_merge,
        grad_up,
        grad_up_bias,
        grad_down,
        grad_down_bias,
        grad_gain,
        grad_bias,
    )
    return (
        block_output,
        grad_tokens,
        summed[0],
        summed[1],
        summed[2],
        summed[3],
        summed[4],
        summed[5],
        summed[6],
        summed[7],
    )


def solution(mesh):
    return jax.shard_map(
        shards,
        mesh=mesh,
        in_specs=(
            P(("dp", "fsdp"), None, None),
            P(("dp", "fsdp"), None),
            P(("dp", "fsdp"), None),
            P(("dp", "fsdp"), None),
            P(("dp", "fsdp")),
            P(("dp", "fsdp"), None),
            P(("dp", "fsdp")),
            P(("dp", "fsdp")),
            P(("dp", "fsdp")),
            P(("dp", "fsdp")),
            P(("dp", "fsdp")),
            P(("dp", "fsdp"), None, None),
        ),
        out_specs=(
            P(("dp", "fsdp"), None, None),
            P(("dp", "fsdp"), None, None),
            P(("dp", "fsdp"), None),
            P(("dp", "fsdp"), None),
            P(("dp", "fsdp"), None),
            P(("dp", "fsdp")),
            P(("dp", "fsdp"), None),
            P(("dp", "fsdp")),
            P(("dp", "fsdp")),
            P(("dp", "fsdp")),
        ),
        check_vma=False,
    )
```

profile of v0, /device:TPU:0, one launch (start us, length us, event | category | flops | bytes accessed | tf_op | source)
XLA Modules:
  0.0 985.5 jit_solution(6889940615130383320)
XLA Ops:
  13.8 42.4 %all-reduce.8 = (bf16[1024]{0:T(1024)(128)(2,1)S(1)}, bf16[1024]{0:T(1024)(128)(2,1)S(1)}, bf16[1024]{0:T(1024)(128)(2,1)S(1)}) all-reduce(bf16[1024]{0:T(1024)(128)(2,1)S(1)} %dynamic-update-slice.1, bf16[1024]{0:T(1024)(128)(2,1)S(1)} %dynamic-update-slice, ...), channel_id=1, replica_groups=mesh['dp'=4,'fsdp'=8] {'dp','fsdp'}, use_global_device_ids=true, to_apply=%add.1 | all-reduce | flops 3072 | bytes 12288
  59.5 23.8 %all-gather.6.cloned.1.call-done = bf16[1024,3072]{1,0:T(8,128)(2,1)} async-done(((bf16[32,3072]{1,0:T(8,128)(2,1)}), bf16[1024,3072]{1,0:T(8,128)(2,1)}) %all-gather.6.cloned.1.call-update) | async-done | bytes 6291472 | tf_op jit(solution)/shard_map/all_gather | solution.py:60
  83.3 5.3 convolution_bitcast_fusion
  92.3 4.2 fusion.69
  113.9 5.1 fusion.32
  123.5 17.8 %all-gather.8.cloned.1.call-done = bf16[1024,1024]{1,0:T(8,128)(2,1)} async-done(((bf16[32,1024]{1,0:T(8,128)(2,1)}), bf16[1024,1024]{1,0:T(8,128)(2,1)}) %all-gather.8.cloned.1.call-update) | async-done | bytes 2097168 | tf_op jit(solution)/shard_map/all_gather | solution.py:61
  144.6 12.0 %multiply_reduce_fusion = (f32[16,416]{1,0:T(8,128)S(1)}, f32[16,416,416]{1,2,0:T(8,128)}) fusion(f32[16,416,416]{1,2,0:T(8,128)} %copy-done, f32[16,416]{1,0:T(8,128)S(1)} %log_add_fusion, pred[416,416]{0,1:T(8,128)(4,1)S(1)} %fusion.44, bf16[416,16,64]{0,2,1:T(8,128)(2,1)S(1)} %bitcast.96, bf16[416,16,64]{0,2,1:T(8,128)(2,1)S(1)} %bitcast.95), kind=kOutput, calls=%fused_computation.1 | convolution fusion | flops 365487616 | bytes 24081408 | tf_op jit(solution)/shard_map/wqhe,wkhe->whqk/dot_general | solution.py:193
  158.5 7.3 multiply_convert_fusion
  174.4 3.4 fusion.33
  177.8 9.8 fusion.36
  188.2 39.5 %all-gather = bf16[32,1,128]{2,1,0:T(2,128)(2,1)S(1)} all-gather(bf16[1,1,128]{2,1,0:T(2,128)(2,1)S(1)} %bitcast.113), channel_id=1, replica_groups=mesh['dp'=4,'fsdp'=8] {'dp','fsdp'}, dimensions={0}, use_global_device_ids=true | all-gather | bytes 8448 | tf_op jit(solution)/shard_map/all_gather | solution.py:63
  227.8 6.5 fusion.65
  237.0 9.0 fusion.38
  246.1 53.4 %all-gather.12.cloned.1.call-done = bf16[4096,1024]{1,0:T(8,128)(2,1)} async-done(((bf16[128,1024]{1,0:T(8,128)(2,1)}), bf16[4096,1024]{1,0:T(8,128)(2,1)}) %all-gather.12.cloned.1.call-update) | async-done | bytes 8388624 | tf_op jit(solution)/shard_map/all_gather | solution.py:64
  299.5 10.8 %convert_reduce_fusion = (f32[4096]{0:T(1024)S(1)}, bf16[416,4096]{1,0:T(8,128)(2,1)S(1)}) fusion(f32[416,4096]{1,0:T(8,128)} %copy-done.25, f32[4096]{0:T(1024)S(1)} %bitcast.111, bf16[4096,1024]{1,0:T(8,128)(2,1)} %all-gather.12.cloned.1.call-done, bf16[1,416,1024]{2,1,0:T(8,128)(2,1)S(1)} %copy-done.20), kind=kOutput, calls=%fused_computation.18 | convolution fusion | flops 3527143424 | bytes 19496960 | tf_op jit(solution)/shard_map/wld,fd->wlf/dot_general | solution.py:176
  311.9 8.3 fusion.62
  320.3 7.6 fusion.71
  327.9 6.8 fusion.27
  336.8 40.1 %all-reduce.7 = (f32[4096]{0:T(1024)S(1)}, f32[1024]{0:T(1024)S(1)}, f32[1024]{0:T(1024)S(1)}, f32[1024]{0:T(1024)S(1)}) all-reduce(f32[4096]{0:T(1024)S(1)} %get-tuple-element.47, f32[1024]{0:T(1024)S(1)} %get-tuple-element.33, f32[1024]{0:T(1024)S(1)} %get-tuple-element.10, ...), channel_id=5, replica_groups=mesh['dp'=4,'fsdp'=8] {'dp','fsdp'}, use_global_device_ids=true, to_apply=%region_11.12.clone | all-reduce | flops 7168 | bytes 57344
  379.2 9.3 fusion.61
  390.7 52.6 %reduce-scatter.7.cloned.1.call-done = f32[32,1024]{1,0:T(8,128)} async-done(((f32[1024,1024]{1,0:T(8,128)}), f32[32,1024]{1,0:T(8,128)}) %reduce-scatter.7.cloned.1.call-update) | async-done | bytes 131088 | tf_op jit(solution)/shard_map/reduce_scatter | solution.py:76
  443.2 158.9 %reduce-scatter.5.cloned.1.call-done = f32[32,3072]{1,0:T(8,128)} async-done(((f32[1024,3072]{1,0:T(8,128)}), f32[32,3072]{1,0:T(8,128)}) %reduce-scatter.5.cloned.1.call-update) | async-done | bytes 393232 | tf_op jit(solution)/shard_map/reduce_scatter | solution.py:75
  602.1 188.7 %reduce-scatter.11.cloned.1.call-done = f32[128,1024]{1,0:T(8,128)} async-done(((f32[4096,1024]{1,0:T(8,128)}), f32[128,1024]{1,0:T(8,128)}) %reduce-scatter.11.cloned.1.call-update) | async-done | bytes 524304 | tf_op jit(solution)/shard_map/reduce_scatter | solution.py:79
  790.9 187.4 %reduce-scatter.9.cloned.1.call-done = f32[32,4096]{1,0:T(8,128)} async-done(((f32[1024,4096]{1,0:T(8,128)}), f32[32,4096]{1,0:T(8,128)}) %reduce-scatter.9.cloned.1.call-update) | async-done | bytes 524304 | tf_op jit(solution)/shard_map/reduce_scatter | solution.py:77
  (141 shorter events, 59.1 us)
Async XLA Ops:
  7.2 76.1 %all-gather.6.cloned.1.call-start = ((), (), s32[]{:S(2)}) async-start(), calls=%async_computation.4 | async-start | bytes 6488064 | tf_op jit(solution)/shard_map/all_gather | solution.py:60
  7.9 133.4 %all-gather.8.cloned.1.call-start = ((), (), s32[]{:S(2)}) async-start(), calls=%async_computation.5 | async-start | bytes 2162688 | tf_op jit(solution)/shard_map/all_gather | solution.py:61
  8.7 219.1 %all-gather.10.cloned.1.call-start = ((), (), s32[]{:S(2)}) async-start(), calls=%async_computation.6 | async-start | bytes 8650752 | tf_op jit(solution)/shard_map/all_gather | solution.py:62
  9.4 290.1 %all-gather.12.cloned.1.call-start = ((), (), s32[]{:S(2)}) async-start(), calls=%async_computation.7 | async-start | bytes 8650752 | tf_op jit(solution)/shard_map/all_gather | solution.py:64
  10.0 433.3 %reduce-scatter.7.cloned.1.call-start = ((), (), s32[]{:S(2)}) async-start(), calls=%async_computation.9 | async-start | bytes 4325376 | tf_op jit(solution)/shard_map/reduce_scatter | solution.py:76
  109.0 4.9 copy-start
  113.9 6.1 copy-start.18
  120.0 21.3 %copy-start.19 = (bf16[1,416,1024]{2,1,0:T(8,128)(2,1)S(1)}, bf16[1,416,1024]{2,1,0:T(8,128)(2,1)}, u32[]{:S(2)}) copy-start(bf16[1,416,1024]{2,1,0:T(8,128)(2,1)} %param.23) | copy-start | bytes 2555908
  123.4 21.1 %copy-start.10 = (bf16[1,416,1024]{1,2,0:T(8,128)(2,1)S(1)}, bf16[1,416,1024]{1,2,0:T(8,128)(2,1)}, u32[]{:S(2)}) copy-start(bf16[1,416,1024]{1,2,0:T(8,128)(2,1)} %copy.54) | copy-start | bytes 2555908
  123.4 478.7 %reduce-scatter.5.cloned.1.call-start = ((), (), s32[]{:S(2)}) async-start(), calls=%async_computation.8 | async-start | bytes 12976128 | tf_op jit(solution)/shard_map/reduce_scatter | solution.py:75
  144.5 12.1 %copy-start.11 = (bf16[416,1024]{0,1:T(8,128)(2,1)}, bf16[416,1024]{0,1:T(8,128)(2,1)S(1)}, u32[]{:S(2)}) copy-start(bf16[416,1024]{0,1:T(8,128)(2,1)S(1)} %copy.62) | copy-start | bytes 2555908
  144.5 12.0 %slice-start = ((s8[13631488]{0:T(1024)(128)(4,1)}), s8[4194304]{0:T(1024)(128)(4,1)S(1)}, s32[]{:S(2)}) async-start(s8[13631488]{0:T(1024)(128)(4,1)} %bitcast.89), calls=%async_computation.12 | async-start | bytes 8388608
  144.6 12.0 %slice-start.1 = ((s8[13631488]{0:T(1024)(128)(4,1)}), s8[4194304]{0:T(1024)(128)(4,1)S(1)}, s32[]{:S(2)}) async-start(s8[13631488]{0:T(1024)(128)(4,1)} %bitcast.89), calls=%async_computation.13 | async-start | bytes 8388608
  144.6 13.7 %slice-start.2 = ((s8[13631488]{0:T(1024)(128)(4,1)}), s8[4194304]{0:T(1024)(128)(4,1)S(1)}, s32[]{:S(2)}) async-start(s8[13631488]{0:T(1024)(128)(4,1)} %bitcast.89), calls=%async_computation.14 | async-start | bytes 8388608
  144.6 13.9 %slice-start.3 = ((s8[13631488]{0:T(1024)(128)(4,1)}), s8[1048576]{0:T(1024)(128)(4,1)S(1)}, s32[]{:S(2)}) async-start(s8[13631488]{0:T(1024)(128)(4,1)} %bitcast.89), calls=%async_computation.15 | async-start | bytes 2097152
  158.5 7.3 copy-start.7
  158.5 7.3 copy-start.9
  187.6 603.3 %reduce-scatter.11.cloned.1.call-start = ((), (), s32[]{:S(2)}) async-start(), calls=%async_computation.11 | async-start | bytes 17301504 | tf_op jit(solution)/shard_map/reduce_scatter | solution.py:79
  227.8 9.3 copy-start.20
  246.0 732.2 %reduce-scatter.9.cloned.1.call-start = ((), (), s32[]{:S(2)}) async-start(), calls=%async_computation.10 | async-start | bytes 17301504 | tf_op jit(solution)/shard_map/reduce_scatter | solution.py:77
  320.3 7.6 copy-start.15
  320.3 7.6 copy-start.17
  379.2 9.4 copy-start.22
  379.2 9.4 copy-start.24
  (15 other events, 35.6 us)
Sparse Core Ops, SparseCore 0:
  11.0 72.2 all-gather.5
  86.3 54.9 all-gather.7
  144.3 76.1 all-gather.9
  223.4 76.0 all-gather.11
  302.2 141.0 reduce-scatter.6
  449.7 152.3 reduce-scatter.4
  605.1 185.7 reduce-scatter.10
  793.8 184.3 reduce-scatter.8
where the time goes:
time: 995 us; the launch traced here: 986 us
  waiting for transfers between devices  685 us (69%)
  blocking collectives  122 us (12%)
  matrix products  108 us (11%)
  local copies, waits for them, and re-layouts  36.2 us (4%)
  other arithmetic  17.8 us (2%)
  between operations  16.5 us (2%)
    reduce_scatter x1, waiting for transfers between devices, reduce_grads(): lax.psum_scatter(grad_down, ('dp', 'fsdp'), scatter_dimension=0, tiled=True)  189 us
    reduce_scatter x1, waiting for transfers between devices, reduce_grads(): lax.psum_scatter(grad_up, ('dp', 'fsdp'), scatter_dimension=0, tiled=True)  187 us
    reduce_scatter x1, waiting for transfers between devices, reduce_grads(): lax.psum_scatter(grad_heads, ('dp', 'fsdp'), scatter_dimension=0, tiled=T...  159 us
    unnamed x2, blocking collectives  82.5 us
    all_gather x1, waiting for transfers between devices, fetch_weights(): lax.all_gather(down_weight, ('dp', 'fsdp'), axis=0, tiled=True)  53.4 us
    reduce_scatter x1, waiting for transfers between devices, reduce_grads(): lax.psum_scatter(grad_merge, ('dp', 'fsdp'), scatter_dimension=0, tiled=T...  52.6 us
    all_gather x1, blocking collectives, fetch_weights(): lax.all_gather(up_bias, ('dp', 'fsdp'), axis=0, tiled=True)  39.5 us
    all_gather x1, waiting for transfers between devices, fetch_weights(): lax.all_gather(heads_weight, ('dp', 'fsdp'), axis=0, tiled=True)  23.8 us
  transfers between devices with their start and end apart: 8, of which 7 were waited for; matrix products, arithmetic and copies ran while one was open for 15% of the time, Pallas kernels for 0%

commit v1 on v0

v1 whole, which is shorter than its diff:
```python
import functools

import jax
import jax.numpy as jnp
import numpy as np
from jax import lax
from jax.experimental import pallas as pl
from jax.experimental.pallas import tpu as pltpu
from jax.sharding import PartitionSpec as P

HEADS = 16
ROT = 32
CORES = 2
GROUP = 4
AXES = ("dp", "fsdp")

eps = 1e-05
big_negative = -1e30
gelu_scale = 0.7978845608028654
gelu_cubic = 0.044715

bf16 = jnp.bfloat16
f32 = jnp.float32


def turn_tables(length, head, lanes):
    position = np.arange(length, dtype=np.float32)
    exponent = np.arange(0, ROT, 2, dtype=np.float32) / np.float32(ROT)
    rate = (np.float32(1.0) / np.power(np.float32(10000.0), exponent)).astype(np.float32)
    phase = (position[:, None] * rate[None, :]).astype(np.float32)
    cosine = np.ones((length, head), np.float32)
    sine = np.zeros((length, head), np.float32)
    cosine[:, :ROT] = np.repeat(np.cos(phase), 2, axis=1)
    sine[:, :ROT] = np.repeat(np.sin(phase), 2, axis=1)
    sine[:, 0:ROT:2] *= -1.0
    copies = lanes // head
    return np.tile(cosine, (1, copies)), np.tile(sine, (1, copies))


def turned(values, cosine, sine):
    lanes = values.shape[1]
    even = lax.broadcasted_iota(jnp.int32, values.shape, 1) % 2 == 0
    other = jnp.where(even, pltpu.roll(values, lanes - 1, 1), pltpu.roll(values, 1, 1))
    return values * cosine + other * sine


def dot(a, b, dims=((1,), (0,))):
    return lax.dot_general(a, b, (dims, ((), ())), preferred_element_type=f32)


def allowed_pairs(offset, end, length):
    key = lax.broadcasted_iota(jnp.int32, (length, 1), 0)
    query = lax.broadcasted_iota(jnp.int32, (1, length), 1)
    key_part = (key >= offset).astype(jnp.int32) + (key > end).astype(jnp.int32)
    query_part = (query >= offset).astype(jnp.int32) + (query > end).astype(jnp.int32)
    return (key_part == query_part) & (query >= key)


def attend_kernel(head, ends_ref, mixed_ref, cos_ref, sin_ref, qkv_ref, att_ref, lse_ref):
    window = pl.program_id(0)
    length, width = mixed_ref.shape
    width = width // 3
    lanes = cos_ref.shape[1]
    allowed = allowed_pairs(ends_ref[window, 0], ends_ref[window, 1], length)
    cosine, sine = cos_ref[...], sin_ref[...]
    lane = lax.broadcasted_iota(jnp.int32, (1, lanes), 1)
    for group in range(width // lanes):
        at = group * lanes
        query = (
            turned(mixed_ref[:, at : at + lanes], cosine, sine) * head ** (-0.5)
        ).astype(bf16)
        keys = turned(mixed_ref[:, width + at : width + at + lanes], cosine, sine).astype(bf16)
        values = mixed_ref[:, 2 * width + at : 2 * width + at + lanes]
        qkv_ref[:, at : at + lanes] = query
        qkv_ref[:, width + at : width + at + lanes] = keys
        qkv_ref[:, 2 * width + at : 2 * width + at + lanes] = values.astype(bf16)
        values_turned = values.T.astype(bf16)
        outs = []
        for sub in range(lanes // head):
            mine = (lane >= sub * head) & (lane < (sub + 1) * head)
            scores = dot(jnp.where(mine, keys, 0), query, ((1,), (1,)))
            scores = jnp.where(allowed, scores, big_negative)
            top = jnp.max(scores, axis=0, keepdims=True)
            expo = jnp.exp(scores - top)
            total = jnp.sum(expo, axis=0, keepdims=True)
            probs = (expo / total).astype(bf16)
            number = group * (lanes // head) + sub
            lse_ref[0, number : number + 1, :] = top + jnp.log(total)
            outs.append(dot(values_turned[sub * head : (sub + 1) * head, :], probs))
        att_ref[:, at : at + lanes] = jnp.concatenate(outs, axis=0).T.astype(bf16)


def attend_back_kernel(
    head, ends_ref, qkv_ref, grad_ref, lse_ref, cos_ref, sin_ref, out_ref
):
    window = pl.program_id(0)
    length, width = qkv_ref.shape
    width = width // 3
    lanes = cos_ref.shape[1]
    allowed = allowed_pairs(ends_ref[window, 0], ends_ref[window, 1], length)
    cosine, sine = cos_ref[...], -sin_ref[...]
    lane = lax.broadcasted_iota(jnp.int32, (1, lanes), 1)
    for group in range(width // lanes):
        at = group * lanes
        query = qkv_ref[:, at : at + lanes]
        keys = qkv_ref[:, width + at : width + at + lanes]
        values = qkv_ref[:, 2 * width + at : 2 * width + at + lanes]
        grad = grad_ref[:, at : at + lanes]
        keys_turned = keys.astype(f32).T.astype(bf16)
        values_grad = jnp.zeros((length, lanes), f32)
        keys_grad = jnp.zeros((length, lanes), f32)
        query_grads = []
        for sub in range(lanes // head):
            mine = (lane >= sub * head) & (lane < (sub + 1) * head)
            number = group * (lanes // head) + sub
            scores = dot(jnp.where(mine, keys, 0), query, ((1,), (1,)))
            probs = jnp.exp(
                jnp.where(allowed, scores, big_negative) - lse_ref[0, number : number + 1, :]
            )
            probs_grad = dot(jnp.where(mine, values, 0), grad, ((1,), (1,)))
            weighted = jnp.sum(probs * probs_grad, axis=0, keepdims=True)
            scores_grad = (probs * (probs_grad - weighted)).astype(bf16)
            values_grad += dot(probs.astype(bf16), jnp.where(mine, grad, 0))
            keys_grad += dot(scores_grad, jnp.where(mine, query, 0))
            query_grads.append(dot(keys_turned[sub * head : (sub + 1) * head, :], scores_grad))
        query_grad = jnp.concatenate(query_grads, axis=0).T * head ** (-0.5)
        out_ref[:, at : at + lanes] = turned(query_grad, cosine, sine).astype(bf16)
        out_ref[:, width + at : width + at + lanes] = turned(keys_grad, cosine, sine).astype(bf16)
        out_ref[:, 2 * width + at : 2 * width + at + lanes] = values_grad.astype(bf16)


def attend(ends, mixed, width, head, length):
    windows = mixed.shape[0] // length
    if (3 * width) % 128:
        mixed = mixed[:, : 3 * width]
    lanes = min(width, 128)
    cosine, sine = turn_tables(length, head, lanes)
    count = max(8, width // head)
    smem = pl.BlockSpec(memory_space=pltpu.SMEM)
    table = pl.BlockSpec((length, lanes), lambda w: (0, 0))
    return pl.pallas_call(
        functools.partial(attend_kernel, head),
        grid=(windows,),
        in_specs=[smem, pl.BlockSpec((length, 3 * width), lambda w: (w, 0)), table, table],
        out_specs=[
            pl.BlockSpec((length, 3 * width), lambda w: (w, 0)),
            pl.BlockSpec((length, width), lambda w: (w, 0)),
            pl.BlockSpec((1, count, length), lambda w: (w, 0, 0)),
        ],
        out_shape=[
            jax.ShapeDtypeStruct((windows * length, 3 * width), bf16),
            jax.ShapeDtypeStruct((windows * length, width), bf16),
            jax.ShapeDtypeStruct((windows, count, length), f32),
        ],
        compiler_params=pltpu.CompilerParams(vmem_limit_bytes=40 * 2**20),
        cost_estimate=pl.CostEstimate(
            flops=windows * 4 * length * length * width,
            bytes_accessed=windows * length * width * 20,
            transcendentals=windows * length * length * (width // head),
        ),
    )(ends, mixed, cosine, sine)


def attend_back(ends, qkv, grad, lse, width, head, length):
    windows = qkv.shape[0] // length
    lanes = min(width, 128)
    cosine, sine = turn_tables(length, head, lanes)
    smem = pl.BlockSpec(memory_space=pltpu.SMEM)
    table = pl.BlockSpec((length, lanes), lambda w: (0, 0))
    return pl.pallas_call(
        functools.partial(attend_back_kernel, head),
        grid=(windows,),
        in_specs=[
            smem,
            pl.BlockSpec((length, 3 * width), lambda w: (w, 0)),
            pl.BlockSpec((length, width), lambda w: (w, 0)),
            pl.BlockSpec((1, lse.shape[1], length), lambda w: (w, 0, 0)),
            table,
            table,
        ],
        out_specs=pl.BlockSpec((length, 3 * width), lambda w: (w, 0)),
        out_shape=jax.ShapeDtypeStruct((windows * length, 3 * width), bf16),
        compiler_params=pltpu.CompilerParams(vmem_limit_bytes=40 * 2**20),
        cost_estimate=pl.CostEstimate(
            flops=windows * 10 * length * length * width,
            bytes_accessed=windows * length * width * 14,
            transcendentals=windows * length * length * (width // head),
        ),
    )(ends, qkv, grad, lse, cosine, sine)


def gelu_tanh(values):
    inner = gelu_scale * (values + gelu_cubic * values * values * values)
    return 0.5 * values * (1.0 + jnp.tanh(inner))


def gelu_slope(values):
    tanh_value = jnp.tanh(gelu_scale * (values + gelu_cubic * values * values * values))
    return 0.5 * (1.0 + tanh_value) + 0.5 * values * (
        1.0 - tanh_value * tanh_value
    ) * gelu_scale * (1.0 + 3.0 * gelu_cubic * values * values)


class Place:
    def __init__(self, sizes):
        self.ndp = sizes["dp"]
        self.no = self.ndp // GROUP
        self.nf = sizes["fsdp"]
        self.nz = self.nf // CORES
        fsdp = lax.axis_index("fsdp")
        self.dp = lax.axis_index("dp")
        self.t = self.dp % GROUP
        self.z = fsdp // CORES
        self.c = fsdp % CORES
        self.outer_groups = [[o * GROUP + t for o in range(self.no)] for t in range(GROUP)]

    def send(self, x, to):
        pairs = []
        for d in range(self.ndp):
            for z in range(self.nz):
                for c in range(CORES):
                    d2, z2, c2 = to(d, z, c)
                    pairs.append(
                        (d * self.nf + z * CORES + c, d2 * self.nf + z2 * CORES + c2)
                    )
        return lax.ppermute(x, AXES, pairs)

    def swap_t(self, x, mask):
        return self.send(x, lambda d, z, c: (d ^ mask, z, c))

    def shift_z(self, x, step=1):
        return self.send(x, lambda d, z, c: (d, (z + step) % self.nz, c))

    def swap_core(self, x):
        return self.send(x, lambda d, z, c: (d, z, CORES - 1 - c))


def later(x, *after):
    return lax.optimization_barrier((x,) + after)[0]


def gather_t(place, x):
    half = x.shape[0] // 2
    one = place.swap_t(x, 1)
    two = place.swap_t(x, 2)
    low = place.swap_t(one[:half], 2)
    high = place.swap_t(two[half:], 1)
    return [x, one, two, low, high]


def sum_t(place, parts):
    half = parts[0].shape[0] // 2
    low = place.swap_t(parts[3][:half], 2)
    high = place.swap_t(parts[3][half:], 1)
    first = jnp.concatenate(
        [(parts[1][:half].astype(f32) + low.astype(f32)).astype(bf16), parts[1][half:]]
    )
    second = jnp.concatenate(
        [parts[2][:half], (parts[2][half:].astype(f32) + high.astype(f32)).astype(bf16)]
    )
    first = place.swap_t(first, 1)
    second = place.swap_t(second, 2)
    return parts[0], first, second


def ring_gather(place, block):
    if place.no > 1:
        block = lax.all_gather(block, "dp", axis_index_groups=place.outer_groups, tiled=True)
    blocks = [block]
    for _ in range(place.nz - 1):
        blocks.append(place.shift_z(blocks[-1]))
    return [[b, place.swap_core(b)] for b in blocks]


def ring_sum(place, parts):
    def add(a, b):
        return a.astype(f32) + b.astype(f32)

    if place.no > 1:
        parts = lax.psum_scatter(
            parts, "dp", scatter_dimension=0, axis_index_groups=place.outer_groups
        )
    else:
        parts = parts[0]
    theirs = lax.dynamic_index_in_dim(parts, 1 - place.c, 1, keepdims=False)
    mine = lax.dynamic_index_in_dim(parts, place.c, 1, keepdims=False)
    chip = add(mine, place.swap_core(theirs)).astype(bf16)

    def at(step):
        return lax.dynamic_index_in_dim(chip, (place.z - step) % place.nz, 0, keepdims=False)

    moving = at(1)
    for step in range(1, place.nz):
        moving = add(place.shift_z(moving), at(step + 1))
        if step < place.nz - 1:
            moving = moving.astype(bf16)
    return moving


def assemble_kernel(layout, steps, place_ref, *refs):
    pieces, out, sem = refs[:-2], refs[-2], refs[-1]
    copies = []
    for number, piece in enumerate(pieces):
        step, flip = number // CORES, number % CORES
        z = place_ref[1] - step
        z = jnp.where(z < 0, z + steps, z)
        c = jnp.bitwise_xor(place_ref[2], flip)
        row, base = 0, 0
        for rows, masks in layout:
            for mask in range(masks):
                d = jnp.bitwise_xor(place_ref[0], mask) if masks > 1 else 0
                to = pl.multiple_of(base + ((d * steps + z) * CORES + c) * rows, rows)
                copies.append(
                    pltpu.make_async_copy(
                        piece.at[pl.ds(row, rows)], out.at[pl.ds(to, rows)], sem.at[len(copies)]
                    )
                )
                row += rows
            base += rows * masks * steps * CORES
    for copy in copies:
        copy.start()
    for copy in copies:
        copy.wait()


def assemble(place, pieces, layout):
    steps = place.nz
    flat = [piece for pair in pieces for piece in pair]
    width = flat[0].shape[1]
    if place.no > 1 or any(r % 16 for r, _ in layout):
        stacked = jnp.stack(flat).reshape(steps, CORES, place.no, -1, width)
        stacked = jnp.take(stacked, (place.z - np.arange(steps)) % steps, axis=0)
        stacked = jnp.take(stacked, np.arange(CORES) ^ place.c, axis=1)
        outs, row = [], 0
        for r, masks in layout:
            part = stacked[:, :, :, row : row + r * masks]
            part = part.reshape(steps, CORES, place.no, masks, r, width)
            if masks > 1:
                part = jnp.take(part, np.arange(masks) ^ place.t, axis=3)
            outs.append(part.transpose(2, 3, 0, 1, 4, 5).reshape(-1, width))
            row += r * masks
        return jnp.concatenate(outs)
    rows = flat[0].shape[0]
    anywhere = pl.BlockSpec(memory_space=pl.ANY)
    count = len(flat) * sum(masks for _, masks in layout)
    return pl.pallas_call(
        functools.partial(assemble_kernel, layout, steps),
        in_specs=[pl.BlockSpec(memory_space=pltpu.SMEM)] + [anywhere] * len(flat),
        out_specs=pl.BlockSpec(memory_space=pltpu.VMEM),
        out_shape=jax.ShapeDtypeStruct((rows * len(flat), width), flat[0].dtype),
        scratch_shapes=[pltpu.SemaphoreType.DMA((count,))],
        compiler_params=pltpu.CompilerParams(vmem_limit_bytes=16 * 2**20),
        cost_estimate=pl.CostEstimate(
            flops=0, bytes_accessed=2 * rows * len(flat) * width * 2, transcendentals=0
        ),
    )(jnp.stack([place.t, place.z, place.c]).astype(jnp.int32), *flat)


def columns(place, heads_weight, up_weight, mask):
    rows, width3 = heads_weight.shape
    part = width3 // 3 // GROUP
    hidden_part = up_weight.shape[1] // GROUP
    to = place.t ^ mask
    joint = [
        lax.dynamic_slice_in_dim(heads_weight, (k * GROUP + to) * part, part, axis=1)
        for k in range(3)
    ]
    up = lax.dynamic_slice_in_dim(up_weight, to * hidden_part, hidden_part, axis=1)
    return jnp.concatenate(joint + [up], axis=1)


def spread(vector, at, count):
    n = vector.shape[0]
    row = jnp.tile(vector.astype(f32).reshape(1, n), (1, count))
    lane = lax.broadcasted_iota(jnp.int32, row.shape, 1)
    return jnp.where(lane // n == at, row, 0.0)


def small_gather(place, norm_gain, norm_bias, down_bias, up_bias, offsets, terminal):
    here = ((place.dp * place.nz) + place.z) * CORES + place.c
    count = place.ndp * place.nf
    rows = jnp.concatenate([spread(v, here, count) for v in (norm_gain, norm_bias, down_bias)])
    fsdp = (place.dp // GROUP * place.nz + place.z) * CORES + place.c
    own = spread(up_bias, fsdp, place.no * place.nf)
    lanes = rows.shape[1]
    both = jnp.concatenate([rows, jnp.pad(own, ((0, 0), (0, lanes - own.shape[1])))])
    if place.no > 1:
        both = lax.psum(both, "dp", axis_index_groups=place.outer_groups)
    shifted = [place.shift_z(both, s) for s in range(1, place.nz)]
    both = sum(shifted, both)
    both = both + place.swap_core(both)
    ends = jnp.concatenate([offsets, terminal]).astype(f32).reshape(1, -1)
    ends = jnp.pad(ends, ((0, 0), (0, lanes - ends.shape[1])))
    group = jnp.concatenate([both[:3], ends])
    others = [place.swap_t(group, m) for m in range(1, GROUP)]
    rows = sum((o[:3] for o in others), group[:3])
    windows = offsets.shape[0]
    ends = jnp.concatenate([g[3:4, : 2 * windows] for g in [group] + others])
    return rows, both[3:4, : own.shape[1]], ends


def shards(
    sizes,
    tokens,
    heads_weight,
    merge_weight,
    up_weight,
    up_bias,
    down_weight,
    down_bias,
    norm_gain,
    norm_bias,
    offsets,
    terminal,
    cotangent,
):
    place = Place(sizes)
    nz, no = place.nz, place.no
    windows, length, width = tokens.shape
    head = width // HEADS
    rows = heads_weight.shape[0]
    hidden_rows = down_weight.shape[0]
    part = width // GROUP
    hidden_part = up_weight.shape[1] // GROUP
    own_rows = windows * length

    own_tokens = tokens.reshape(own_rows, width)
    token_pieces = gather_t(place, own_tokens)
    own_grad = cotangent.reshape(own_rows, width)
    grad_pieces = gather_t(place, later(own_grad, token_pieces[1], token_pieces[2]))

    pieces = [
        columns(place, heads_weight, up_weight, m) for m in range(GROUP)
    ]
    pieces = [pieces[0]] + [place.swap_t(pieces[m], m) for m in range(1, GROUP)]
    heads_up = assemble(place, ring_gather(place, jnp.concatenate(pieces)), [(rows, GROUP)])
    down_merge = assemble(
        place,
        ring_gather(place, jnp.concatenate([down_weight, merge_weight])),
        [(hidden_rows, 1), (rows, 1)],
    )

    small, up_shift, ends = small_gather(
        place, norm_gain, norm_bias, down_bias, up_bias, offsets, terminal
    )
    gain_full, shift_full, down_shift = small[0:1], small[1:2], small[2:3]
    ends = ends.reshape(GROUP, 2, windows).swapaxes(1, 2).reshape(GROUP * windows, 2)
    ends = ends.astype(jnp.int32)

    all_tokens = jnp.concatenate(token_pieces)
    grad = jnp.concatenate(grad_pieces)

    def normalised(values):
        values = values.astype(f32)
        centered = values - jnp.mean(values, axis=-1, keepdims=True)
        inverse_std = lax.rsqrt(jnp.mean(centered * centered, axis=-1, keepdims=True) + eps)
        return centered * inverse_std, inverse_std

    normed, _ = normalised(all_tokens)
    acts = (normed * gain_full + shift_full).astype(bf16)
    mixed_hidden = dot(acts, heads_up)
    qkv, attended, lse = attend(ends, mixed_hidden, part, head, length)
    hidden = mixed_hidden[:, 3 * part :] + up_shift
    activated = gelu_tanh(hidden).astype(bf16)
    joined = jnp.concatenate([activated, attended], axis=1)
    out_terms = dot(joined, down_merge).astype(bf16).reshape(GROUP, own_rows, width)
    out_sum = sum((t.astype(f32) for t in sum_t(place, [out_terms[m] for m in range(GROUP)])), 0.0)
    block_output = (own_tokens.astype(f32) + out_sum + down_shift).astype(bf16)

    joined_grad = dot(grad, down_merge, ((1,), (1,)))
    hidden_grad = (joined_grad[:, :hidden_part] * gelu_slope(hidden)).astype(bf16)
    attended_grad = joined_grad[:, hidden_part:].astype(bf16)
    grad_down_merge = dot(joined, grad, ((0,), (0,))).astype(bf16)
    mixed_grad = attend_back(ends, qkv, attended_grad, lse, part, head, length)
    both_grad = jnp.concatenate([mixed_grad, hidden_grad], axis=1)
    acts_grad = dot(both_grad, heads_up, ((1,), (1,)))
    grad_heads_up = dot(acts, both_grad, ((0,), (0,))).astype(bf16)

    grad_gain = jnp.sum(acts_grad * normed, axis=0)
    grad_bias = jnp.sum(acts_grad, axis=0)
    grad_down_bias = jnp.sum(grad.astype(f32), axis=0)
    grad_up_bias = jnp.sum(hidden_grad.astype(f32), axis=0)
    per_row = hidden_rows // rows
    up_rows = grad_up_bias.reshape(no, 1, nz, CORES, rows, per_row)
    up_rows = jnp.broadcast_to(up_rows, (no, GROUP, nz, CORES, rows, per_row))
    up_rows = up_rows.reshape(width, per_row)
    extra = jnp.concatenate(
        [grad_gain[:, None], grad_bias[:, None], grad_down_bias[:, None], up_rows], axis=1
    ).astype(bf16)
    extra = jnp.pad(extra, ((0, 0), (0, 128 - extra.shape[1])))

    acts_terms = acts_grad.astype(bf16).reshape(GROUP, own_rows, width)
    acts_sum = sum((t.astype(f32) for t in sum_t(place, [acts_terms[m] for m in range(GROUP)])), 0.0)
    own_normed, inverse_std = normalised(own_tokens)
    normed_grad = acts_sum * gain_full
    grad_tokens = (
        own_grad.astype(f32)
        + inverse_std
        * (
            normed_grad
            - jnp.mean(normed_grad, axis=-1, keepdims=True)
            - own_normed * jnp.mean(normed_grad * own_normed, axis=-1, keepdims=True)
        )
    ).astype(bf16)

    down_terms = grad_down_merge[:hidden_part].reshape(no, nz, CORES, hidden_rows, width)
    merge_terms = grad_down_merge[hidden_part:].reshape(no, nz, CORES, rows, width)
    down_merge_sum = ring_sum(place, jnp.concatenate([down_terms, merge_terms], axis=3))
    grad_down, grad_merge = down_merge_sum[:hidden_rows], down_merge_sum[hidden_rows:]

    terms = jnp.concatenate([grad_heads_up, extra], axis=1)
    terms = terms.reshape(no, GROUP, nz, CORES, rows, terms.shape[1]).transpose(0, 2, 3, 1, 4, 5)
    summed = ring_sum(place, terms).astype(bf16)

    def block(mask):
        return lax.dynamic_index_in_dim(summed, place.t ^ mask, 0, keepdims=False)

    arrived = [block(0)] + [place.swap_t(block(m), m) for m in range(1, GROUP)]
    by_t = []
    for t in range(GROUP):
        mask = t ^ place.t
        by_t.append(lax.select_n(mask, *arrived).astype(f32))
    grad_heads = jnp.concatenate(
        [b[:, k * part : (k + 1) * part] for k in range(3) for b in by_t], axis=1
    )
    grad_up = jnp.concatenate([b[:, 3 * part : 3 * part + hidden_part] for b in by_t], axis=1)
    last = [a[:, 3 * part + hidden_part :].astype(f32) for a in arrived]
    return (
        block_output.reshape(tokens.shape),
        grad_tokens.reshape(tokens.shape),
        grad_heads,
        grad_merge,
        grad_up,
        last[0][:, 3 : 3 + per_row].reshape(-1),
        grad_down,
        last[0][:, 2],
        sum(a[:, 0] for a in last),
        sum(a[:, 1] for a in last),
    )


def solution(mesh):
    whole = P(AXES)
    return jax.shard_map(
        functools.partial(shards, dict(mesh.shape)),
        mesh=mesh,
        in_specs=(whole,) * 12,
        out_specs=(whole,) * 10,
        check_vma=False,
    )
```

time: 995 us -> 320 us (0.32)
  waiting for transfers between devices: 685 us -> 140 us
  blocking collectives: 122 us -> 0 us
  matrix products: 108 us -> 46 us
  starting transfers between devices: 0.32 us -> 42.3 us
  Pallas kernels: 0 us -> 32.2 us
  local copies, waits for them, and re-layouts: 36.2 us -> 20.5 us
  between operations: 16.5 us -> 3.47 us
  other arithmetic: 17.8 us -> 30.7 us
    reduce_scatter x4 -> x0, waiting for transfers between devices: 588 us -> none  [the longest x1 189 us: reduce_grads(): lax.psum_scatter(grad_down, ('dp', 'fsdp'), scatter_dimension=0, tiled=True)]
    ppermute x0 -> x51, waiting for transfers between devices: none -> 140 us  [send(): return lax.ppermute(x, AXES, pairs)]
    all_gather x4 -> x0, waiting for transfers between devices: 95 us -> none  [the longest x1 53.4 us: fetch_weights(): lax.all_gather(down_weight, ('dp', 'fsdp'), axis=0, tiled=True)]
    unnamed x2 -> x0, blocking collectives: 82.5 us -> none
    dot_general x18 -> x6, matrix products: 108 us -> 46 us  [dot(): return lax.dot_general(a, b, (dims, ((), ())), preferred_element_type=f32)]
    ppermute x0 -> x51, starting transfers between devices: none -> 42.3 us  [send(): return lax.ppermute(x, AXES, pairs)]
    all_gather x1 -> x0, blocking collectives: 39.5 us -> none  [fetch_weights(): lax.all_gather(up_bias, ('dp', 'fsdp'), axis=0, tiled=True)]
    pallas_call x0 -> x4, Pallas kernels: none -> 32.2 us  [the longest x1 13.7 us: attend_back(): pl.pallas_call(functools.partial(attend_back_kernel, head), grid=(windows...]
  transfers between devices with their start and end apart: 8 -> 51, of which waited for: 7 -> 19; matrix products, arithmetic and copies ran while one was open for 15% -> 27% of each run, Pallas kernels for 0% -> 10%
where the time goes in v1:
time: 320 us; the launch traced here: 316 us
  waiting for transfers between devices  140 us (44%)
  matrix products  46 us (14%)
  starting transfers between devices  42.3 us (13%)
  Pallas kernels  32.2 us (10%)
  other arithmetic  30.7 us (10%)
  local copies, waits for them, and re-layouts  20.5 us (6%)
  between operations  3.47 us (1%)
    ppermute x51, waiting for transfers between devices, send(): return lax.ppermute(x, AXES, pairs)  140 us
    dot_general x6, matrix products, dot(): return lax.dot_general(a, b, (dims, ((), ())), preferred_element_type=f32)  46 us
    ppermute x51, starting transfers between devices, send(): return lax.ppermute(x, AXES, pairs)  42.3 us
    pallas_call x1, Pallas kernels, attend_back(): pl.pallas_call(functools.partial(attend_back_kernel, head), grid=(windows...  13.7 us
    pallas_call x1, Pallas kernels, attend(): pl.pallas_call(functools.partial(attend_kernel, head), grid=(windows,), i...  10.4 us
    unnamed x60, local copies, waits for them, and re-layouts  8.35 us
    pallas_call x2, Pallas kernels, assemble(): pl.pallas_call(functools.partial(assemble_kernel, layout, steps), in_spec...  8.11 us
  transfers between devices with their start and end apart: 51, of which 19 were waited for; matrix products, arithmetic and copies ran while one was open for 27% of the time, Pallas kernels for 10%

profile of v1, /device:TPU:0, one launch (start us, length us, event | category | flops | bytes accessed | tf_op | source)
XLA Modules:
  0.0 315.6 jit_solution(13733306213284903869)
XLA Ops:
  25.6 6.5 %collective-permute-done.10 = f32[4,1024]{1,0:T(4,128)S(1)} collective-permute-done((f32[4,1024]{1,0:T(4,128)S(1)}, f32[4,1024]{1,0:T(4,128)S(1)}, u32[]{:S(2)}, u32[]{:S(2)}) %collective-permute-start.10) | collective-permute-done | bytes 16416 | tf_op jit(solution)/shard_map/ppermute | solution.py:226
  42.2 5.7 %collective-permute-done.22.refs_2_ = bf16[160,1024]{1,0:T(8,128)(2,1)S(1)} collective-permute-done((bf16[160,1024]{1,0:T(8,128)(2,1)S(1)}, bf16[160,1024]{1,0:T(8,128)(2,1)S(1)}, u32[]{:S(2)}, u32[]{:S(2)}) %collective-permute-start.22) | collective-permute-done | bytes 327712 | tf_op jit(solution)/shard_map/ppermute | solution.py:226
  52.0 5.8 %collective-permute-done.15.refs_2_ = bf16[128,1792]{1,0:T(8,128)(2,1)S(1)} collective-permute-done((bf16[128,1792]{1,0:T(8,128)(2,1)S(1)}, bf16[128,1792]{1,0:T(8,128)(2,1)S(1)}, u32[]{:S(2)}, u32[]{:S(2)}) %collective-permute-start.15) | collective-permute-done | bytes 458784 | tf_op jit(solution)/shard_map/ppermute | solution.py:226
  57.8 4.8 %collective-permute-done.24.refs_4_ = bf16[160,1024]{1,0:T(8,128)(2,1)S(1)} collective-permute-done((bf16[160,1024]{1,0:T(8,128)(2,1)S(1)}, bf16[160,1024]{1,0:T(8,128)(2,1)S(1)}, u32[]{:S(2)}, u32[]{:S(2)}) %collective-permute-start.24) | collective-permute-done | bytes 327712 | tf_op jit(solution)/shard_map/ppermute | solution.py:226
  65.7 16.1 %collective-permute-done.26.refs_6_ = bf16[160,1024]{1,0:T(8,128)(2,1)S(1)} collective-permute-done((bf16[160,1024]{1,0:T(8,128)(2,1)S(1)}, bf16[160,1024]{1,0:T(8,128)(2,1)S(1)}, u32[]{:S(2)}, u32[]{:S(2)}) %collective-permute-start.26) | collective-permute-done | bytes 327712 | tf_op jit(solution)/shard_map/ppermute | solution.py:226
  85.6 11.3 %collective-permute-done.19.refs_6_ = bf16[128,1792]{1,0:T(8,128)(2,1)S(1)} collective-permute-done((bf16[128,1792]{1,0:T(8,128)(2,1)S(1)}, bf16[128,1792]{1,0:T(8,128)(2,1)S(1)}, u32[]{:S(2)}, u32[]{:S(2)}) %collective-permute-start.19) | collective-permute-done | bytes 458784 | tf_op jit(solution)/shard_map/ppermute | solution.py:226
  102.2 6.5 %shard_map.231 = bf16[1024,1792]{1,0:T(8,128)(2,1)S(1)} custom-call(s32[3]{0:T(128)S(1)} %pad_add_fusion.place_ref, bf16[128,1792]{1,0:T(8,128)(2,1)S(1)} %pad_maximum_fusion.13.refs_0_, bf16[128,1792]{1,0:T(8,128)(2,1)S(1)} %collective-permute-done.14.refs_1_, bf16[128,1792]{1,0:T(8,128)(2,1)S(1)} %collective-permute-done.15.refs_2_, ...), custom_call_target="tpu_custom_call" | custom-call | bytes 7340032 | tf_op jit(solution)/shard_map/pallas_call | solution.py:346
  108.7 7.0 %fusion.54.mixed_ref = f32[1664,1792]{1,0:T(8,128)S(1)} fusion(bf16[1024,1792]{1,0:T(8,128)(2,1)S(1)} %shard_map.231, bf16[1664,1024]{1,0:T(8,128)(2,1)S(1)} %constant_dynamic-update-slice_fusion, f32[1024]{0:T(1024)S(1)} %bitcast.117, f32[1024]{0:T(1024)S(1)} %bitcast.111, f32[1664]{0:T(1024)S(1)} %add_rsqrt_fusion, f32[1664]{0:T(1024)S(1)} %broadcast_multiply_fusion), kind=kOutput, calls=%fused_computation.185 | convolution fusion | flops 6117130240 | bytes 19026944 | tf_op jit(solution)/shard_map/dot_general | solution.py:48
  115.7 4.2 %multiply_convert_fusion = bf16[1664,1024]{1,0:T(8,128)(2,1)} fusion(f32[1664,1792]{1,0:T(8,128)S(1)} %fusion.54.mixed_ref, f32[1024]{0:T(1024)S(1)} %bitcast.109), kind=kLoop, calls=%fused_computation.22 | loop fusion | flops 17039360 | bytes 10227712 | tf_op jit(solution)/shard_map/convert_element_type | solution.py:464
  121.1 10.4 %shard_map.232 = (bf16[1664,768]{1,0:T(8,128)(2,1)S(1)}, bf16[1664,256]{1,0:T(8,128)(2,1)S(1)}, f32[4,8,416]{2,1,0:T(8,128)S(1)}) custom-call(s32[4,2]{1,0:T(4,128)S(1)} %maximum_convert_fusion.ends_ref, f32[1664,1792]{1,0:T(8,128)} %copy-done.2, f32[416,128]{1,0:T(8,128)S(1)} %copy-done.1, f32[416,128]{1,0:T(8,128)S(1)} %copy-done), custom_call_target="tpu_custom_call" | custom-call | flops 708837376 | bytes 8519680 | tf_op jit(solution)/shard_map/pallas_call | solution.py:141
  131.5 7.0 %convolution_convert_fusion.1 = bf16[1664,1024]{1,0:T(8,128)(2,1)S(1)} fusion(bf16[1280,1024]{1,0:T(8,128)(2,1)S(1)} %shard_map.233, bf16[1664,256]{1,0:T(8,128)(2,1)S(1)} %get-tuple-element.14, bf16[1664,1024]{1,0:T(8,128)(2,1)} %multiply_convert_fusion), kind=kOutput, calls=%fused_computation.32 | convolution fusion | flops 4372299776 | bytes 10289152 | tf_op jit(solution)/shard_map/dot_general | solution.py:48
  145.3 6.8 %fusion.66 = f32[1664,1280]{1,0:T(8,128)S(1)} fusion(bf16[1664,1024]{1,0:T(8,128)(2,1)} %get-tuple-element.59, bf16[1280,1024]{1,0:T(8,128)(2,1)S(1)} %shard_map.233), kind=kOutput, calls=%fused_computation.195 | convolution fusion | flops 4362076160 | bytes 14548992 | tf_op jit(solution)/shard_map/dot_general | solution.py:48
  152.2 5.9 %fusion.56 = (bf16[1024]{0:T(1024)(128)(2,1)S(1)}, bf16[1664,1024]{1,0:T(8,128)(2,1)}) fusion(f32[1024]{0:T(1024)S(1)} %bitcast.110, f32[1664,1792]{1,0:T(8,128)S(1)} %bitcast.96, f32[1664,1280]{1,0:T(8,128)S(1)} %fusion.66), kind=kLoop, calls=%fused_computation.186 | loop fusion | flops 35781632 | bytes 17045504 | tf_op jit(solution)/shard_map/reduce_sum | solution.py:482
  158.1 13.7 %shard_map.234 = bf16[1664,768]{1,0:T(8,128)(2,1)S(1)} custom-call(s32[4,2]{1,0:T(4,128)S(1)} %maximum_convert_fusion.ends_ref, bf16[1664,768]{1,0:T(8,128)(2,1)S(1)} %get-tuple-element.15.qkv_ref, bf16[1664,256]{1,0:T(8,128)(2,1)S(1)} %slice.434.grad_ref, f32[4,8,416]{2,1,0:T(8,128)S(1)} %get-tuple-element.17.lse_ref, f32[416,128]{1,0:T(8,128)S(1)} %copy-done.1, ...), custom_call_target="tpu_custom_call" | custom-call | flops 1772093440 | bytes 5963776 | tf_op jit(solution)/shard_map/pallas_call | solution.py:170
  171.8 10.0 %fusion.7 = (bf16[1024]{0:T(1024)(128)(2,1)S(1)}, bf16[1024]{0:T(1024)(128)(2,1)S(1)}, bf16[1664,1024]{1,0:T(8,128)(2,1)}) fusion(bf16[1664,1024]{1,0:T(8,128)(2,1)S(1)} %copy-done.6, f32[1664]{0:T(1024)S(1)} %add_rsqrt_fusion, f32[1664]{0:T(1024)S(1)} %broadcast_multiply_fusion, bf16[1024,1792]{1,0:T(8,128)(2,1)S(1)} %shard_map.231, ...), kind=kOutput, calls=%fused_computation.12 | convolution fusion | flops 6130759680 | bytes 16466944 | tf_op jit(solution)/shard_map/dot_general | solution.py:48
  181.9 9.6 %fusion.20 = bf16[1024,1792]{1,0:T(8,128)(2,1)} fusion(bf16[1664,1024]{1,0:T(8,128)(2,1)S(1)} %copy-done.8, bf16[1664,768]{1,0:T(8,128)(2,1)S(1)} %shard_map.234, bf16[1664,1024]{1,0:T(8,128)(2,1)S(1)} %copy-done.6, f32[1024]{0:T(1024)S(1)} %bitcast.118, f32[1024]{0:T(1024)S(1)} %bitcast.112, f32[1664]{0:T(1024)S(1)} %add_rsqrt_fusion, ...), kind=kOutput, calls=%fused_computation.30 | convolution fusion | flops 6130892800 | bytes 13063168 | tf_op jit(solution)/shard_map/dot_general | solution.py:48
  197.5 5.6 %convolution_convert_fusion = bf16[1280,1024]{1,0:T(8,128)(2,1)S(1)} fusion(bf16[1664,1024]{1,0:T(8,128)(2,1)S(1)} %copy-done.16, bf16[1664,256]{1,0:T(8,128)(2,1)S(1)} %get-tuple-element.14, bf16[1664,1024]{1,0:T(8,128)(2,1)S(1)} %copy-done.12), kind=kOutput, calls=%fused_computation.31 | convolution fusion | flops 4371906560 | bytes 10289152 | tf_op jit(solution)/shard_map/dot_general | solution.py:48
  210.6 7.4 %collective-permute-done.36 = bf16[208,1024]{1,0:T(8,128)(2,1)S(1)} collective-permute-done((bf16[208,1024]{1,0:T(8,128)(2,1)S(1)}, bf16[208,1024]{1,0:T(8,128)(2,1)S(1)}, u32[]{:S(2)}, u32[]{:S(2)}) %collective-permute-start.36) | collective-permute-done | bytes 426016 | tf_op jit(solution)/shard_map/ppermute | solution.py:226
  223.3 29.4 %collective-permute-done.39 = bf16[416,1024]{1,0:T(8,128)(2,1)S(1)} collective-permute-done((bf16[416,1024]{1,0:T(8,128)(2,1)S(1)}, bf16[416,1024]{1,0:T(8,128)(2,1)S(1)}, u32[]{:S(2)}, u32[]{:S(2)}) %collective-permute-start.39) | collective-permute-done | bytes 852000 | tf_op jit(solution)/shard_map/ppermute | solution.py:226
  254.1 14.5 %collective-permute-done.41 = bf16[4,32,1920]{2,1,0:T(8,128)(2,1)S(1)} collective-permute-done((bf16[4,32,1920]{2,1,0:T(8,128)(2,1)S(1)}, bf16[4,32,1920]{2,1,0:T(8,128)(2,1)S(1)}, u32[]{:S(2)}, u32[]{:S(2)}) %collective-permute-start.41) | collective-permute-done | bytes 491552 | tf_op jit(solution)/shard_map/ppermute | solution.py:226
  268.8 6.8 %collective-permute-done.48 = bf16[160,1024]{1,0:T(8,128)(2,1)S(1)} collective-permute-done((bf16[160,1024]{1,0:T(8,128)(2,1)S(1)}, bf16[160,1024]{1,0:T(8,128)(2,1)S(1)}, u32[]{:S(2)}, u32[]{:S(2)}) %collective-permute-start.48) | collective-permute-done | bytes 327712 | tf_op jit(solution)/shard_map/ppermute | solution.py:226
  275.8 10.4 %collective-permute-done.42 = bf16[4,32,1920]{2,1,0:T(8,128)(2,1)S(1)} collective-permute-done((bf16[4,32,1920]{2,1,0:T(8,128)(2,1)S(1)}, bf16[4,32,1920]{2,1,0:T(8,128)(2,1)S(1)}, u32[]{:S(2)}, u32[]{:S(2)}) %collective-permute-start.42) | collective-permute-done | bytes 491552 | tf_op jit(solution)/shard_map/ppermute | solution.py:226
  288.7 4.4 %collective-permute-done.49 = bf16[160,1024]{1,0:T(8,128)(2,1)S(1)} collective-permute-done((bf16[160,1024]{1,0:T(8,128)(2,1)S(1)}, bf16[160,1024]{1,0:T(8,128)(2,1)S(1)}, u32[]{:S(2)}, u32[]{:S(2)}) %collective-permute-start.49) | collective-permute-done | bytes 327712 | tf_op jit(solution)/shard_map/ppermute | solution.py:226
  293.3 10.4 %collective-permute-done.43 = bf16[4,32,1920]{2,1,0:T(8,128)(2,1)S(1)} collective-permute-done((bf16[4,32,1920]{2,1,0:T(8,128)(2,1)S(1)}, bf16[4,32,1920]{2,1,0:T(8,128)(2,1)S(1)}, u32[]{:S(2)}, u32[]{:S(2)}) %collective-permute-start.43) | collective-permute-done | bytes 491552 | tf_op jit(solution)/shard_map/ppermute | solution.py:226
  (254 shorter events, 92.0 us)
Async XLA Ops:
  10.4 37.5 %collective-permute-start = (bf16[416,1024]{1,0:T(8,128)(2,1)}, bf16[416,1024]{1,0:T(8,128)(2,1)S(1)}, u32[]{:S(2)}, u32[]{:S(2)}) collective-permute-start(bf16[416,1024]{1,0:T(8,128)(2,1)} %bitcast.97), channel_id=1, source_target_pairs={{0,8},{1,9},{2,10},{3,11},{4,12},{5,13},{6,14},{7,15},{8,0},{9,1},... | collective-permute-start | bytes 2555912 | tf_op jit(solution)/shard_map/ppermute | solution.py:226
  11.9 36.1 %collective-permute-start.1 = (bf16[416,1024]{1,0:T(8,128)(2,1)}, bf16[416,1024]{1,0:T(8,128)(2,1)}, u32[]{:S(2)}, u32[]{:S(2)}) collective-permute-start(bf16[416,1024]{1,0:T(8,128)(2,1)} %bitcast.98), channel_id=1, source_target_pairs={{0,16},{1,17},{2,18},{3,19},{4,20},{5,21},{6,22},{7,23},{8,24},{9,... | collective-permute-start | bytes 2555912 | tf_op jit(solution)/shard_map/ppermute | solution.py:226
  38.5 25.3 %collective-permute-start.21 = (bf16[160,1024]{1,0:T(8,128)(2,1)S(1)}, bf16[160,1024]{1,0:T(8,128)(2,1)S(1)}, u32[]{:S(2)}, u32[]{:S(2)}) collective-permute-start(bf16[160,1024]{1,0:T(8,128)(2,1)S(1)} %constant_dynamic-update-slice_fusion.5.refs_0_), channel_id=1, source_target_pairs={{0,1},{1,0},{2,3},{3,2},{4,5},{5,4},{6,7},{7,6},{8,9},{9,8},{10,11... | collective-permute-start | bytes 983048 | tf_op jit(solution)/shard_map/ppermute | solution.py:226
  62.6 19.2 %collective-permute-start.17 = (bf16[128,1792]{1,0:T(8,128)(2,1)S(1)}, bf16[128,1792]{1,0:T(8,128)(2,1)S(1)}, u32[]{:S(2)}, u32[]{:S(2)}) collective-permute-start(bf16[128,1792]{1,0:T(8,128)(2,1)S(1)} %collective-permute-done.15.refs_2_), channel_id=1, source_target_pairs={{0,2},{1,3},{2,4},{3,5},{4,6},{5,7},{6,0},{7,1},{8,10},{9,11},{10,... | collective-permute-start | bytes 1376264 | tf_op jit(solution)/shard_map/ppermute | solution.py:226
  62.6 19.2 %collective-permute-start.26 = (bf16[160,1024]{1,0:T(8,128)(2,1)S(1)}, bf16[160,1024]{1,0:T(8,128)(2,1)S(1)}, u32[]{:S(2)}, u32[]{:S(2)}) collective-permute-start(bf16[160,1024]{1,0:T(8,128)(2,1)S(1)} %collective-permute-done.24.refs_4_), channel_id=1, source_target_pairs={{0,2},{1,3},{2,4},{3,5},{4,6},{5,7},{6,0},{7,1},{8,10},{9,11},{10,... | collective-permute-start | bytes 983048 | tf_op jit(solution)/shard_map/ppermute | solution.py:226
  62.7 34.3 %collective-permute-start.33 = (bf16[416,1024]{1,0:T(8,128)(2,1)S(1)}, bf16[416,1024]{1,0:T(8,128)(2,1)S(1)}, u32[]{:S(2)}, u32[]{:S(2)}) collective-permute-start(bf16[416,1024]{1,0:T(8,128)(2,1)S(1)} %bitcast.106), channel_id=1, source_target_pairs={{0,16},{1,17},{2,18},{3,19},{4,20},{5,21},{6,22},{7,23},{8,24},{9,... | collective-permute-start | bytes 2555912 | tf_op jit(solution)/shard_map/ppermute | solution.py:226
  63.8 34.4 %collective-permute-start.32 = (bf16[416,1024]{1,0:T(8,128)(2,1)S(1)}, bf16[416,1024]{1,0:T(8,128)(2,1)S(1)}, u32[]{:S(2)}, u32[]{:S(2)}) collective-permute-start(bf16[416,1024]{1,0:T(8,128)(2,1)S(1)} %bitcast.107), channel_id=1, source_target_pairs={{0,8},{1,9},{2,10},{3,11},{4,12},{5,13},{6,14},{7,15},{8,0},{9,1},... | collective-permute-start | bytes 2555912 | tf_op jit(solution)/shard_map/ppermute | solution.py:226
  65.6 17.7 %collective-permute-start.25 = (bf16[160,1024]{1,0:T(8,128)(2,1)S(1)}, bf16[160,1024]{1,0:T(8,128)(2,1)S(1)}, u32[]{:S(2)}, u32[]{:S(2)}) collective-permute-start(bf16[160,1024]{1,0:T(8,128)(2,1)S(1)} %collective-permute-done.24.refs_4_), channel_id=1, source_target_pairs={{0,1},{1,0},{2,3},{3,2},{4,5},{5,4},{6,7},{7,6},{8,9},{9,8},{10,11... | collective-permute-start | bytes 983048 | tf_op jit(solution)/shard_map/ppermute | solution.py:226
  83.3 17.5 %collective-permute-start.14 = (bf16[128,1792]{1,0:T(8,128)(2,1)S(1)}, bf16[128,1792]{1,0:T(8,128)(2,1)S(1)}, u32[]{:S(2)}, u32[]{:S(2)}) collective-permute-start(bf16[128,1792]{1,0:T(8,128)(2,1)S(1)} %pad_maximum_fusion.13.refs_0_), channel_id=1, source_target_pairs={{0,1},{1,0},{2,3},{3,2},{4,5},{5,4},{6,7},{7,6},{8,9},{9,8},{10,11... | collective-permute-start | bytes 1376264 | tf_op jit(solution)/shard_map/ppermute | solution.py:226
  83.9 18.3 %collective-permute-start.16 = (bf16[128,1792]{1,0:T(8,128)(2,1)S(1)}, bf16[128,1792]{1,0:T(8,128)(2,1)S(1)}, u32[]{:S(2)}, u32[]{:S(2)}) collective-permute-start(bf16[128,1792]{1,0:T(8,128)(2,1)S(1)} %collective-permute-done.15.refs_2_), channel_id=1, source_target_pairs={{0,1},{1,0},{2,3},{3,2},{4,5},{5,4},{6,7},{7,6},{8,9},{9,8},{10,11... | collective-permute-start | bytes 1376264 | tf_op jit(solution)/shard_map/ppermute | solution.py:226
  98.3 45.0 %collective-permute-start.35 = (bf16[208,1024]{1,0:T(8,128)(2,1)}, bf16[208,1024]{1,0:T(8,128)(2,1)}, u32[]{:S(2)}, u32[]{:S(2)}) collective-permute-start(bf16[208,1024]{1,0:T(8,128)(2,1)} %slice.320), channel_id=1, source_target_pairs={{0,8},{1,9},{2,10},{3,11},{4,12},{5,13},{6,14},{7,15},{8,0},{9,1},... | collective-permute-start | bytes 1277960 | tf_op jit(solution)/shard_map/ppermute | solution.py:226
  100.8 40.6 %collective-permute-start.34 = (bf16[208,1024]{1,0:T(8,128)(2,1)}, bf16[208,1024]{1,0:T(8,128)(2,1)}, u32[]{:S(2)}, u32[]{:S(2)}) collective-permute-start(bf16[208,1024]{1,0:T(8,128)(2,1)} %slice.319), channel_id=1, source_target_pairs={{0,16},{1,17},{2,18},{3,19},{4,20},{5,21},{6,22},{7,23},{8,24},{9,... | collective-permute-start | bytes 1277960 | tf_op jit(solution)/shard_map/ppermute | solution.py:226
  139.7 68.0 %collective-permute-start.28 = (bf16[208,1024]{1,0:T(8,128)(2,1)}, bf16[208,1024]{1,0:T(8,128)(2,1)}, u32[]{:S(2)}, u32[]{:S(2)}) collective-permute-start(bf16[208,1024]{1,0:T(8,128)(2,1)} %get-tuple-element.38), channel_id=1, source_target_pairs={{0,16},{1,17},{2,18},{3,19},{4,20},{5,21},{6,22},{7,23},{8,24},{9,... | collective-permute-start | bytes 1277960 | tf_op jit(solution)/shard_map/ppermute | solution.py:226
  140.4 67.4 %collective-permute-start.30 = (bf16[208,1024]{1,0:T(8,128)(2,1)}, bf16[208,1024]{1,0:T(8,128)(2,1)}, u32[]{:S(2)}, u32[]{:S(2)}) collective-permute-start(bf16[208,1024]{1,0:T(8,128)(2,1)} %get-tuple-element.39), channel_id=1, source_target_pairs={{0,8},{1,9},{2,10},{3,11},{4,12},{5,13},{6,14},{7,15},{8,0},{9,1},... | collective-permute-start | bytes 1277960 | tf_op jit(solution)/shard_map/ppermute | solution.py:226
  195.5 25.5 %collective-permute-start.40 = (bf16[4,4,32,1920]{3,2,0,1:T(8,128)(2,1)S(1)}, bf16[4,4,32,1920]{3,2,0,1:T(8,128)(2,1)S(1)}, u32[]{:S(2)}, u32[]{:S(2)}) collective-permute-start(bf16[4,4,32,1920]{3,2,0,1:T(8,128)(2,1)S(1)} %dynamic-slice_bitcast_fusion), channel_id=1, source_target_pairs={{0,1},{1,0},{2,3},{3,2},{4,5},{5,4},{6,7},{7,6},{8,9},{9,8},{10,11... | collective-permute-start | bytes 5898248 | tf_op jit(solution)/shard_map/ppermute | solution.py:226
  207.7 45.7 %collective-permute-start.47 = (bf16[4,160,1024]{2,1,0:T(8,128)(2,1)S(1)}, bf16[4,160,1024]{2,1,0:T(8,128)(2,1)S(1)}, u32[]{:S(2)}, u32[]{:S(2)}) collective-permute-start(bf16[4,160,1024]{2,1,0:T(8,128)(2,1)S(1)} %fusion.35), channel_id=1, source_target_pairs={{0,1},{1,0},{2,3},{3,2},{4,5},{5,4},{6,7},{7,6},{8,9},{9,8},{10,11... | collective-permute-start | bytes 3932168 | tf_op jit(solution)/shard_map/ppermute | solution.py:226
  209.4 77.0 %collective-permute-start.31 = (bf16[416,1024]{1,0:T(8,128)(2,1)S(1)}, bf16[416,1024]{1,0:T(8,128)(2,1)S(1)}, u32[]{:S(2)}, u32[]{:S(2)}) collective-permute-start(bf16[416,1024]{1,0:T(8,128)(2,1)S(1)} %pad_maximum_fusion.9), channel_id=1, source_target_pairs={{0,16},{1,17},{2,18},{3,19},{4,20},{5,21},{6,22},{7,23},{8,24},{9,... | collective-permute-start | bytes 2555912 | tf_op jit(solution)/shard_map/ppermute | solution.py:226
  218.4 34.2 %collective-permute-start.39 = (bf16[416,1024]{1,0:T(8,128)(2,1)S(1)}, bf16[416,1024]{1,0:T(8,128)(2,1)S(1)}, u32[]{:S(2)}, u32[]{:S(2)}) collective-permute-start(bf16[416,1024]{1,0:T(8,128)(2,1)S(1)} %pad_maximum_fusion.11), channel_id=1, source_target_pairs={{0,16},{1,17},{2,18},{3,19},{4,20},{5,21},{6,22},{7,23},{8,24},{9,... | collective-permute-start | bytes 2555912 | tf_op jit(solution)/shard_map/ppermute | solution.py:226
  220.5 32.1 %collective-permute-start.37 = (bf16[416,1024]{1,0:T(8,128)(2,1)S(1)}, bf16[416,1024]{1,0:T(8,128)(2,1)S(1)}, u32[]{:S(2)}, u32[]{:S(2)}) collective-permute-start(bf16[416,1024]{1,0:T(8,128)(2,1)S(1)} %pad_maximum_fusion.10), channel_id=1, source_target_pairs={{0,8},{1,9},{2,10},{3,11},{4,12},{5,13},{6,14},{7,15},{8,0},{9,1},... | collective-permute-start | bytes 2555912 | tf_op jit(solution)/shard_map/ppermute | solution.py:226
  221.0 65.3 %collective-permute-start.29 = (bf16[416,1024]{1,0:T(8,128)(2,1)S(1)}, bf16[416,1024]{1,0:T(8,128)(2,1)S(1)}, u32[]{:S(2)}, u32[]{:S(2)}) collective-permute-start(bf16[416,1024]{1,0:T(8,128)(2,1)S(1)} %pad_maximum_fusion.8), channel_id=1, source_target_pairs={{0,8},{1,9},{2,10},{3,11},{4,12},{5,13},{6,14},{7,15},{8,0},{9,1},... | collective-permute-start | bytes 2555912 | tf_op jit(solution)/shard_map/ppermute | solution.py:226
  254.1 21.6 %collective-permute-start.48 = (bf16[160,1024]{1,0:T(8,128)(2,1)S(1)}, bf16[160,1024]{1,0:T(8,128)(2,1)S(1)}, u32[]{:S(2)}, u32[]{:S(2)}) collective-permute-start(bf16[160,1024]{1,0:T(8,128)(2,1)S(1)} %dynamic-slice_bitcast_fusion.2), channel_id=1, source_target_pairs={{0,2},{1,3},{2,4},{3,5},{4,6},{5,7},{6,0},{7,1},{8,10},{9,11},{10,... | collective-permute-start | bytes 983048 | tf_op jit(solution)/shard_map/ppermute | solution.py:226
  268.7 17.4 %collective-permute-start.42 = (bf16[4,32,1920]{2,1,0:T(8,128)(2,1)S(1)}, bf16[4,32,1920]{2,1,0:T(8,128)(2,1)S(1)}, u32[]{:S(2)}, u32[]{:S(2)}) collective-permute-start(bf16[4,32,1920]{2,1,0:T(8,128)(2,1)S(1)} %fusion.40), channel_id=1, source_target_pairs={{0,2},{1,3},{2,4},{3,5},{4,6},{5,7},{6,0},{7,1},{8,10},{9,11},{10,... | collective-permute-start | bytes 1474568 | tf_op jit(solution)/shard_map/ppermute | solution.py:226
  275.7 17.5 %collective-permute-start.49 = (bf16[160,1024]{1,0:T(8,128)(2,1)S(1)}, bf16[160,1024]{1,0:T(8,128)(2,1)S(1)}, u32[]{:S(2)}, u32[]{:S(2)}) collective-permute-start(bf16[160,1024]{1,0:T(8,128)(2,1)S(1)} %fusion.44), channel_id=1, source_target_pairs={{0,2},{1,3},{2,4},{3,5},{4,6},{5,7},{6,0},{7,1},{8,10},{9,11},{10,... | collective-permute-start | bytes 983048 | tf_op jit(solution)/shard_map/ppermute | solution.py:226
  286.3 17.4 %collective-permute-start.43 = (bf16[4,32,1920]{2,1,0:T(8,128)(2,1)S(1)}, bf16[4,32,1920]{2,1,0:T(8,128)(2,1)S(1)}, u32[]{:S(2)}, u32[]{:S(2)}) collective-permute-start(bf16[4,32,1920]{2,1,0:T(8,128)(2,1)S(1)} %fusion.39), channel_id=1, source_target_pairs={{0,2},{1,3},{2,4},{3,5},{4,6},{5,7},{6,0},{7,1},{8,10},{9,11},{10,... | collective-permute-start | bytes 1474568 | tf_op jit(solution)/shard_map/ppermute | solution.py:226
  (49 other events, 524.7 us)

commit v2 on v1

v2 whole, which is shorter than its diff:
```python
import functools

import jax
import jax.numpy as jnp
import numpy as np
from jax import lax
from jax.experimental import pallas as pl
from jax.experimental.pallas import tpu as pltpu
from jax.sharding import PartitionSpec as P

HEADS = 16
ROT = 32
CORES = 2
GROUP = 4
AXES = ("dp", "fsdp")

eps = 1e-05
big_negative = -1e30
gelu_scale = 0.7978845608028654
gelu_cubic = 0.044715

bf16 = jnp.bfloat16
f32 = jnp.float32


def turn_tables(length, head, lanes):
    position = np.arange(length, dtype=np.float32)
    exponent = np.arange(0, ROT, 2, dtype=np.float32) / np.float32(ROT)
    rate = (np.float32(1.0) / np.power(np.float32(10000.0), exponent)).astype(np.float32)
    phase = (position[:, None] * rate[None, :]).astype(np.float32)
    cosine = np.ones((length, head), np.float32)
    sine = np.zeros((length, head), np.float32)
    cosine[:, :ROT] = np.repeat(np.cos(phase), 2, axis=1)
    sine[:, :ROT] = np.repeat(np.sin(phase), 2, axis=1)
    sine[:, 0:ROT:2] *= -1.0
    copies = lanes // head
    return np.tile(cosine, (1, copies)), np.tile(sine, (1, copies))


def turned(values, cosine, sine):
    lanes = values.shape[1]
    even = lax.broadcasted_iota(jnp.int32, values.shape, 1) % 2 == 0
    other = jnp.where(even, pltpu.roll(values, lanes - 1, 1), pltpu.roll(values, 1, 1))
    return values * cosine + other * sine


def dot(a, b, dims=((1,), (0,))):
    return lax.dot_general(a, b, (dims, ((), ())), preferred_element_type=f32)


def allowed_pairs(ends, length):
    offset = (16.0 * ends[:, 0:1] + ends[:, 1:2]).astype(jnp.int32)
    end = (16.0 * ends[:, 2:3] + ends[:, 3:4]).astype(jnp.int32)
    key = lax.broadcasted_iota(jnp.int32, (length, 1), 0)
    query = lax.broadcasted_iota(jnp.int32, (1, length), 1)
    key_part = (key >= offset).astype(jnp.int32) + (key > end).astype(jnp.int32)
    query_part = (query >= offset).astype(jnp.int32) + (query > end).astype(jnp.int32)
    return (key_part == query_part) & (query >= key)


def spec(space):
    return pl.BlockSpec(memory_space=space)


def settings(mebibytes):
    return {
        "compiler_params": pltpu.CompilerParams(vmem_limit_bytes=mebibytes * 2**20),
        "cost_estimate": pl.CostEstimate(flops=1, bytes_accessed=1, transcendentals=0),
    }


TICK = jax.ShapeDtypeStruct((8, 128), jnp.float32)


def tick(ref):
    ref[...] = jnp.zeros_like(ref)


def call(kernel, ins, outs, mebibytes, after=(), scratch=()):
    many = len(ins)

    def body(*refs):
        rest = refs[many + len(after) :]
        tick(rest[len(outs)])
        kernel(*refs[:many], *rest[: len(outs)], *rest[len(outs) + 1 :])

    result = pl.pallas_call(
        body,
        in_specs=[spec(pltpu.SMEM if x.dtype == jnp.int32 else pltpu.VMEM) for x in ins]
        + [spec(pl.ANY)] * len(after),
        out_specs=[spec(pltpu.VMEM)] * (len(outs) + 1),
        out_shape=[*outs, TICK],
        scratch_shapes=list(scratch),
        **settings(mebibytes),
    )(*ins, *after)
    return result[:-1], result[-1]


def shape16(*dims):
    return jax.ShapeDtypeStruct(dims, bf16)


def stacked(refs):
    return jnp.concatenate([r[...] for r in refs])


def normalised(values):
    mean = jnp.mean(values, axis=-1, keepdims=True)
    centered = values - mean
    inverse_std = lax.rsqrt(jnp.mean(centered * centered, axis=-1, keepdims=True) + eps)
    return centered * inverse_std, inverse_std


def gelu_and_slope(h):
    square = h * h
    tanh_value = jnp.tanh(h * (gelu_scale + gelu_scale * gelu_cubic * square))
    half = 0.5 * (1.0 + tanh_value)
    slope = half + (0.5 * h) * (1.0 - tanh_value * tanh_value) * (
        gelu_scale + 3.0 * gelu_scale * gelu_cubic * square
    )
    return h * half, slope


def ends_of(window, ends_ref):
    rows, width = ends_ref.shape
    at = rows // GROUP * window
    return ends_ref[at : at + 16, width - 128 :].astype(f32)[4:5]


def attend_kernel(head, window, ends_ref, heads_ref, small_ref, cos_ref, sin_ref, *refs):
    tokens = refs[:2]
    acts_ref, normed_ref, attended_ref, qkv_ref, lse_ref = refs[2:]
    length, part = attended_ref.shape
    lanes = cos_ref.shape[1]
    normed, _ = normalised(stacked(tokens).astype(f32))
    normed_ref[...] = normed.astype(bf16)
    acts_ref[...] = (normed * small_ref[0:1, :] + small_ref[1:2, :]).astype(bf16)
    acts = acts_ref[...]
    query_all, keys_all, values_all = (
        dot(acts, heads_ref[:, k * part : (k + 1) * part]) for k in range(3)
    )
    allowed = allowed_pairs(ends_of(window, ends_ref), length)
    cosine, sine = cos_ref[...], sin_ref[...]
    lane = lax.broadcasted_iota(jnp.int32, (1, lanes), 1)
    for group in range(part // lanes):
        at = group * lanes
        query = (turned(query_all[:, at : at + lanes], cosine, sine) * head ** (-0.5)).astype(bf16)
        keys = turned(keys_all[:, at : at + lanes], cosine, sine).astype(bf16)
        values = values_all[:, at : at + lanes]
        qkv_ref[:, at : at + lanes] = query
        qkv_ref[:, part + at : part + at + lanes] = keys
        qkv_ref[:, 2 * part + at : 2 * part + at + lanes] = values.astype(bf16)
        values_turned = values.T.astype(bf16)
        outs = []
        for sub in range(lanes // head):
            mine = (lane >= sub * head) & (lane < (sub + 1) * head)
            scores = dot(jnp.where(mine, keys, 0), query, ((1,), (1,)))
            scores = jnp.where(allowed, scores, big_negative)
            top = jnp.max(scores, axis=0, keepdims=True)
            expo = jnp.exp(scores - top)
            total = jnp.sum(expo, axis=0, keepdims=True)
            probs = (expo * (1.0 / total)).astype(bf16)
            number = group * (lanes // head) + sub
            lse_ref[number : number + 1, :] = top + jnp.log(total)
            outs.append(dot(values_turned[sub * head : (sub + 1) * head, :], probs))
        attended_ref[:, at : at + lanes] = jnp.concatenate(outs, axis=0).T.astype(bf16)


def attend(window, ends, tokens, heads, small, tables, head, after=()):
    length, width = 2 * tokens[0].shape[0], tokens[0].shape[1]
    part = heads.shape[1] // 3
    outs = [shape16(length, w) for w in (width, width, part, 3 * part)]
    outs.append(jax.ShapeDtypeStruct((max(8, part // head), length), f32))
    kernel = functools.partial(attend_kernel, head, window)
    return call(kernel, [ends, heads, small, *tables, *tokens], outs, 6, after)


def hidden_kernel(up_ref, small_ref, acts_ref, activated_ref, slope_ref):
    acts = acts_ref[...]
    hidden_part = up_ref.shape[1]
    step = min(256, hidden_part)
    for at in range(0, hidden_part, step):
        hidden = dot(acts, up_ref[:, at : at + step])
        value, slope = gelu_and_slope(hidden + small_ref[3:4, at : at + step])
        activated_ref[:, at : at + step] = value.astype(bf16)
        slope_ref[:, at : at + step] = slope.astype(bf16)


def hidden_units(acts, up, small, after=()):
    outs = [shape16(acts.shape[0], up.shape[1])] * 2
    return call(hidden_kernel, [up, small, acts], outs, 4, after)


def out_kernel(down_ref, merge_ref, activated_ref, attended_ref, low_ref, high_ref):
    half, width = low_ref.shape
    activated, attended = activated_ref[...], attended_ref[...]
    step = min(256, width)
    for at in range(0, width, step):
        term = dot(activated, down_ref[:, at : at + step])
        term = (term + dot(attended, merge_ref[:, at : at + step])).astype(bf16)
        low_ref[:, at : at + step] = term[:half]
        high_ref[:, at : at + step] = term[half:]


def out_terms(activated, attended, down, merge, after=()):
    outs = [shape16(activated.shape[0] // 2, down.shape[1])] * 2
    return call(out_kernel, [down, merge, activated, attended], outs, 4, after)


def joined_grad_kernel(
    down_ref, merge_ref, slope_ref, low_ref, high_ref, hidden_ref, attended_ref, sums_ref
):
    hidden_part = hidden_ref.shape[1]
    grad = stacked([low_ref, high_ref])
    sums_ref[...] = jnp.zeros_like(sums_ref)
    sums_ref[0:1, :] = jnp.sum(grad.astype(f32), axis=0, keepdims=True)
    step = min(256, hidden_part)
    for at in range(0, hidden_part, step):
        term = dot(grad, down_ref[at : at + step, :], ((1,), (1,)))
        term = (term * slope_ref[:, at : at + step].astype(f32)).astype(bf16)
        hidden_ref[:, at : at + step] = term
        sums_ref[1:2, at : at + step] = jnp.sum(term.astype(f32), axis=0, keepdims=True)
    attended_ref[...] = dot(grad, merge_ref[...], ((1,), (1,))).astype(bf16)


def joined_grad(grad, down, merge, slope, after=()):
    length, hidden_part = slope.shape
    outs = [shape16(length, hidden_part), shape16(length, merge.shape[0])]
    outs.append(jax.ShapeDtypeStruct((8, max(down.shape)), f32))
    return call(joined_grad_kernel, [down, merge, slope, *grad], outs, 5, after)


def attend_back_kernel(
    head, window, ends_ref, cos_ref, sin_ref, qkv_ref, grad_ref, lse_ref, mixed_ref
):
    length = qkv_ref.shape[0]
    part = qkv_ref.shape[1] // 3
    lanes = cos_ref.shape[1]
    allowed = allowed_pairs(ends_of(window, ends_ref), length)
    cosine, sine = cos_ref[...], -sin_ref[...]
    lane = lax.broadcasted_iota(jnp.int32, (1, lanes), 1)
    for group in range(part // lanes):
        at = group * lanes
        query = qkv_ref[:, at : at + lanes]
        keys = qkv_ref[:, part + at : part + at + lanes]
        values = qkv_ref[:, 2 * part + at : 2 * part + at + lanes]
        grad = grad_ref[:, at : at + lanes]
        keys_turned = keys.astype(f32).T.astype(bf16)
        values_grad = jnp.zeros((length, lanes), f32)
        keys_grad = jnp.zeros((length, lanes), f32)
        query_grads = []
        for sub in range(lanes // head):
            mine = (lane >= sub * head) & (lane < (sub + 1) * head)
            number = group * (lanes // head) + sub
            scores = dot(jnp.where(mine, keys, 0), query, ((1,), (1,)))
            probs = jnp.exp(
                jnp.where(allowed, scores, big_negative) - lse_ref[number : number + 1, :]
            )
            probs_grad = dot(jnp.where(mine, values, 0), grad, ((1,), (1,)))
            weighted = jnp.sum(probs * probs_grad, axis=0, keepdims=True)
            scores_grad = (probs * (probs_grad - weighted)).astype(bf16)
            values_grad += dot(probs.astype(bf16), jnp.where(mine, grad, 0))
            keys_grad += dot(scores_grad, jnp.where(mine, query, 0))
            query_grads.append(dot(keys_turned[sub * head : (sub + 1) * head, :], scores_grad))
        query_grad = jnp.concatenate(query_grads, axis=0).T * head ** (-0.5)
        mixed_ref[:, at : at + lanes] = turned(query_grad, cosine, sine).astype(bf16)
        mixed_ref[:, part + at : part + at + lanes] = turned(keys_grad, cosine, sine).astype(bf16)
        mixed_ref[:, 2 * part + at : 2 * part + at + lanes] = values_grad.astype(bf16)


def attend_back(window, ends, qkv, grad, lse, tables, head, after=()):
    kernel = functools.partial(attend_back_kernel, head, window)
    return call(kernel, [ends, *tables, qkv, grad, lse], [shape16(*qkv.shape)], 6, after)


def acts_grad_kernel(
    heads_ref, up_ref, mixed_ref, hidden_ref, normed_ref, low_ref, high_ref, sums_ref
):
    mixed, hidden = mixed_ref[...], hidden_ref[...]
    half, width = low_ref.shape
    step = min(256, width)
    sums_ref[...] = jnp.zeros_like(sums_ref)
    for at in range(0, width, step):
        term = dot(mixed, heads_ref[at : at + step, :], ((1,), (1,)))
        term += dot(hidden, up_ref[at : at + step, :], ((1,), (1,)))
        sums_ref[0:1, at : at + step] = jnp.sum(
            term * normed_ref[:, at : at + step].astype(f32), axis=0, keepdims=True
        )
        sums_ref[1:2, at : at + step] = jnp.sum(term, axis=0, keepdims=True)
        low_ref[:, at : at + step] = term[:half].astype(bf16)
        high_ref[:, at : at + step] = term[half:].astype(bf16)


def acts_grad(heads, up, mixed, hidden, normed, after=()):
    length, width = normed.shape
    outs = [shape16(length // 2, width)] * 2 + [jax.ShapeDtypeStruct((8, width), f32)]
    (low, high, sums), done = call(
        acts_grad_kernel, [heads, up, mixed, hidden, normed], outs, 5, after
    )
    return (low, high), sums, done


def joined_windows(refs, scratch):
    at = 0
    for ref in refs:
        rows = ref.shape[0]
        scratch[at : at + rows, :] = ref[...]
        at += rows


def row_grads_kernel(rows, place_ref, *refs):
    activated, attended, grads = refs[:GROUP], refs[GROUP : 2 * GROUP], refs[2 * GROUP : 4 * GROUP]
    theirs_ref, mine_ref, a_ref, b_ref, g_ref = refs[4 * GROUP :]
    joined_windows(activated, a_ref)
    joined_windows(attended, b_ref)
    joined_windows(grads, g_ref)
    first = place_ref[2] == 0
    grad = g_ref[...]
    at = 0
    for ref, size in ((a_ref, theirs_ref.shape[1] - rows), (b_ref, rows)):
        step = min(256, ref.shape[1])
        for start in range(0, ref.shape[1], step):
            term = dot(ref[:, start : start + step], grad, ((0,), (0,))).astype(bf16)
            for pair in range(step // (CORES * size)):
                z = start // (CORES * size) + pair
                zero = term[pair * 2 * size : (pair * 2 + 1) * size]
                one = term[(pair * 2 + 1) * size : (pair * 2 + 2) * size]
                mine_ref[z, at : at + size, :] = jnp.where(first, zero, one)
                theirs_ref[z, at : at + size, :] = jnp.where(first, one, zero)
        at += size


def row_grads(where, steps, rows, activated, attended, grads, after=()):
    length, hidden_part = activated[0].shape
    part = attended[0].shape[1]
    width = grads[0].shape[1]
    out = shape16(steps, hidden_part // (steps * CORES) + rows, width)
    scratch = [pltpu.VMEM((GROUP * length, w), bf16) for w in (hidden_part, part, width)]
    ins = [where, *activated, *attended, *grads]
    kernel = functools.partial(row_grads_kernel, rows)
    return call(kernel, ins, [out, out], 12, after, scratch)


def column_grads_kernel(rows, place_ref, *refs):
    theirs_ref, mine_ref, a_ref, b_ref = refs[2 * GROUP :]
    steps = theirs_ref.shape[0]
    joined_windows(refs[:GROUP], a_ref)
    joined_windows(refs[GROUP : 2 * GROUP], b_ref)
    first = place_ref[2] == 0
    grad = b_ref[...]
    step = steps * CORES * rows
    for t in range(GROUP):
        term = dot(a_ref[:, t * step : (t + 1) * step], grad, ((0,), (0,))).astype(bf16)
        for z in range(steps):
            zero = term[z * 2 * rows : (z * 2 + 1) * rows]
            one = term[(z * 2 + 1) * rows : (z * 2 + 2) * rows]
            mine_ref[z, t * rows : (t + 1) * rows, :] = jnp.where(first, zero, one)
            theirs_ref[z, t * rows : (t + 1) * rows, :] = jnp.where(first, one, zero)


def column_grads(where, steps, rows, acts, grads, after=()):
    length, width = acts[0].shape
    columns = grads[0].shape[1]
    out = shape16(steps, GROUP * rows, columns)
    scratch = [pltpu.VMEM((GROUP * length, w), bf16) for w in (width, columns)]
    kernel = functools.partial(column_grads_kernel, rows)
    return call(kernel, [where, *acts, *grads], [out, out], 12, after, scratch)


def ring_begin_kernel(steps, place_ref, mine_ref, got_ref, chip_ref, first_ref):
    for z in range(steps):
        chip_ref[z] = (mine_ref[z].astype(f32) + got_ref[z].astype(f32)).astype(bf16)
    at = lax.rem(place_ref[1] + steps - 1, steps)
    first_ref[...] = chip_ref[at]


def ring_add_kernel(steps, step, place_ref, chip_ref, moving_ref, out_ref):
    at = lax.rem(place_ref[1] + 2 * steps - step, steps)
    out_ref[...] = (chip_ref[at].astype(f32) + moving_ref[...].astype(f32)).astype(bf16)


def ring_rows_kernel(place_ref, chip_ref, moving_ref, down_ref, merge_ref):
    total = chip_ref[place_ref[1]].astype(f32) + moving_ref[...].astype(f32)
    size = down_ref.shape[0]
    down_ref[...] = total[:size]
    merge_ref[...] = total[size:]


def ring_columns_kernel(place_ref, chip_ref, moving_ref, *outs):
    rows = outs[0].shape[0]
    for mask in range(GROUP):
        t = jnp.bitwise_xor(place_ref[0], mask)
        at = pl.ds(pl.multiple_of(t * rows, rows), rows)
        total = chip_ref[place_ref[1], at, :].astype(f32) + moving_ref[at, :].astype(f32)
        outs[mask][...] = total.astype(bf16)


def add_pairs_kernel(*refs):
    for i in range(len(refs) // 3):
        a, b, out = refs[2 * i], refs[2 * i + 1], refs[len(refs) // 3 * 2 + i]
        out[...] = (a[...].astype(f32) + b[...].astype(f32)).astype(bf16)


def add_pairs(*arrays, after=()):
    outs = [shape16(*a.shape) for a in arrays[::2]]
    return call(add_pairs_kernel, list(arrays), outs, 3, after)


def small_sums_kernel(*refs):
    out_ref = refs[-1]
    count = len(refs) // 2
    out_ref[...] = jnp.zeros_like(out_ref)
    out_ref[0:2, :] = sum((r[0:2, :] for r in refs[1:count]), refs[0][0:2, :])
    out_ref[2:4, :] = sum((r[0:2, :] for r in refs[count + 1 : -1]), refs[count][0:2, :])


def summed_halves(own, one, two, scratch):
    half = own[0].shape[0]
    for i in range(2):
        scratch[i * half : (i + 1) * half, :] = (
            own[i][...].astype(f32) + one[i][...].astype(f32) + two[i][...].astype(f32)
        )


def finish_out_kernel(low_ref, high_ref, small_ref, *refs):
    out_ref, scratch = refs[-2:]
    summed_halves(refs[0:2], refs[2:4], refs[4:6], scratch)
    tokens = stacked([low_ref, high_ref]).astype(f32)
    out_ref[...] = (tokens + scratch[...] + small_ref[2:3, :]).astype(bf16)


def finish_grad_kernel(low_ref, high_ref, grad_low_ref, grad_high_ref, small_ref, *refs):
    out_ref, scratch = refs[-2:]
    summed_halves(refs[0:2], refs[2:4], refs[4:6], scratch)
    normed, inverse_std = normalised(stacked([low_ref, high_ref]).astype(f32))
    normed_grad = scratch[...] * small_ref[0:1, :]
    mean = jnp.mean(normed_grad, axis=-1, keepdims=True)
    along = jnp.mean(normed_grad * normed, axis=-1, keepdims=True)
    grad = stacked([grad_low_ref, grad_high_ref]).astype(f32)
    out_ref[...] = (grad + inverse_std * (normed_grad - mean - normed * along)).astype(bf16)


def finish(kernel, arrays, terms, after=()):
    flat = [half for pair in terms for half in pair]
    half, width = flat[0].shape
    scratch = [pltpu.VMEM((2 * half, width), f32)]
    (out,), _ = call(kernel, [*arrays, *flat], [shape16(2 * half, width)], 8, after, scratch)
    return out


def prepare_kernel(
    place_ref, ends_ref, small_ref, heads_ref, up_ref, down_ref, merge_ref, tokens_ref, grad_ref, *refs
):
    outs, halves, tick_ref, sem = refs[: GROUP + 1], refs[GROUP + 1 : -2], refs[-2], refs[-1]
    rows = heads_ref.shape[0]
    part = heads_ref.shape[1] // 3 // GROUP
    hidden_part = up_ref.shape[1] // GROUP
    hidden_rows = down_ref.shape[0]
    copies = []

    def copy(src, dst):
        copies.append(pltpu.make_async_copy(src, dst, sem.at[len(copies)]))

    for mask in range(GROUP):
        to = jnp.bitwise_xor(place_ref[0], mask)
        for k in range(3):
            at = pl.multiple_of((k * GROUP + to) * part, part)
            copy(heads_ref.at[:, pl.ds(at, part)], outs[mask].at[:, pl.ds(k * part, part)])
        at = pl.multiple_of(to * hidden_part, hidden_part)
        copy(
            up_ref.at[:, pl.ds(at, hidden_part)],
            outs[mask].at[:, pl.ds(3 * part + 128, hidden_part)],
        )
    copy(down_ref, outs[GROUP].at[pl.ds(0, hidden_rows)])
    copy(merge_ref, outs[GROUP].at[pl.ds(hidden_rows, rows)])
    size = halves[0].shape[0]
    for i, half in enumerate(halves):
        copy((tokens_ref, grad_ref)[i // 2].at[pl.ds(i % 2 * size, size)], half)
    for each in copies:
        each.start()
    tick(tick_ref)
    quarter = place_ref[3]
    row = lax.broadcasted_iota(jnp.int32, (rows, 128), 0)
    lane = lax.broadcasted_iota(jnp.int32, (rows, 128), 1)
    first = jnp.broadcast_to(small_ref[0:1, :], (rows, 128))
    extra = jnp.zeros((rows, 128), f32)
    for k in range(3):
        moved = pltpu.roll(first, lax.rem(quarter * rows + (128 - k * rows), 128), 1)
        here = (row == k) & (lane >= quarter * rows) & (lane < (quarter + 1) * rows)
        extra = jnp.where(here, moved, extra)
    extra = jnp.where(row == 3, small_ref[1:2, :], extra)
    for k in range(2):
        value = ends_ref[k]
        for i, piece in enumerate((value // 16, value % 16)):
            extra = jnp.where((row == 4) & (lane == 2 * k + i), piece.astype(f32), extra)
    extra = extra.astype(bf16)
    for mask in range(GROUP):
        outs[mask][:, 3 * part : 3 * part + 128] = extra
    for each in copies:
        each.wait()


def prepare(where, ends, small, heads_weight, up_weight, down_weight, merge_weight, tokens, grad):
    rows, width3 = heads_weight.shape
    columns = width3 // GROUP + up_weight.shape[1] // GROUP + 128
    block = (down_weight.shape[0] + merge_weight.shape[0], down_weight.shape[1])
    half = (tokens.shape[0] // 2, tokens.shape[1])
    far = [heads_weight, up_weight, down_weight, merge_weight, tokens, grad]
    far = [pltpu.with_memory_space_constraint(x, pltpu.HBM) for x in far]
    return pl.pallas_call(
        prepare_kernel,
        in_specs=[spec(pltpu.SMEM)] * 2 + [spec(pltpu.VMEM)] + [spec(pltpu.HBM)] * len(far),
        out_specs=[spec(pltpu.VMEM)] * (GROUP + 6),
        out_shape=[shape16(rows, columns)] * GROUP + [shape16(*block)] + [shape16(*half)] * 4 + [TICK],
        scratch_shapes=[pltpu.SemaphoreType.DMA((4 * GROUP + 6,))],
        **settings(2),
    )(where, ends, small, *far)


def small_rows_kernel(count, place_ref, extra_ref, small_ref):
    total = extra_ref.shape[0]
    rows = total // (count * GROUP)
    row = lax.broadcasted_iota(jnp.int32, (8, 128), 0)
    per = 128 // rows
    for tile in range(small_ref.shape[1] // 128):
        value = jnp.zeros((8, 128), f32)
        for i in range(per):
            at = (tile * per + i) * rows
            value += extra_ref[at : at + 16, :].astype(f32)[:8]
        if tile < count:
            at = pl.multiple_of((place_ref[0] * count + tile) * rows, rows)
            value = jnp.where(row == 3, extra_ref[pl.ds(at, 16), :].astype(f32)[:8], value)
        small_ref[:, tile * 128 : (tile + 1) * 128] = value


def assemble_kernel(layout, steps, with_small, place_ref, *refs):
    count = steps * CORES
    pieces = refs[:count]
    outs = refs[-1 - len(layout) - 2 * with_small :]
    sem = refs[-1]
    copies = []

    def copy(src, dst):
        copies.append(pltpu.make_async_copy(src, dst, sem.at[len(copies)]))

    for number, piece in enumerate(pieces):
        z = place_ref[1] - number // CORES
        z = jnp.where(z < 0, z + steps, z)
        c = jnp.bitwise_xor(place_ref[2], number % CORES)
        row = 0
        for (rows, masks), out in zip(layout, outs):
            width = out.shape[1]
            for mask in range(masks):
                d = jnp.bitwise_xor(place_ref[0], mask) if masks > 1 else 0
                to = pl.ds(pl.multiple_of(((d * steps + z) * CORES + c) * rows, rows), rows)
                source = piece.at[pl.ds(row, rows)]
                if with_small:
                    copy(source.at[:, pl.ds(0, width)], out.at[to])
                    copy(source.at[:, pl.ds(width, 128)], refs[-2].at[to])
                else:
                    copy(source, out.at[to])
                row += rows
    for each in copies:
        each.start()
    for each in copies:
        each.wait()
    if with_small:
        small_rows_kernel(count, place_ref, refs[-2], outs[len(layout)])


def assemble(place, where, pieces, layout, with_small=False, after=()):
    steps = place.nz
    flat = [piece for pair in pieces for piece in pair]
    width = flat[0].shape[1]
    if place.no > 1 or any(r % 16 for r, _ in layout):
        stacked_pieces = jnp.stack(flat).reshape(steps, CORES, place.no, -1, width)
        stacked_pieces = jnp.take(stacked_pieces, (place.z - np.arange(steps)) % steps, axis=0)
        stacked_pieces = jnp.take(stacked_pieces, np.arange(CORES) ^ place.c, axis=1)
        outs, row = [], 0
        for r, masks in layout:
            part = stacked_pieces[:, :, :, row : row + r * masks]
            part = part.reshape(steps, CORES, place.no, masks, r, width)
            if masks > 1:
                part = jnp.take(part, np.arange(masks) ^ place.t, axis=3)
            outs.append(part.transpose(2, 3, 0, 1, 4, 5).reshape(-1, width))
            row += r * masks
        return outs
    if with_small:
        width -= 128
    count = len(flat) * sum(masks for _, masks in layout) * (2 if with_small else 1)
    totals = [len(flat) * r * masks for r, masks in layout]
    shapes = [jax.ShapeDtypeStruct((total, width), bf16) for total in totals]
    scratch = [pltpu.SemaphoreType.DMA((count,))]
    if with_small:
        shapes.append(jax.ShapeDtypeStruct((8, totals[0]), f32))
        scratch.insert(0, pltpu.VMEM((totals[0], 128), bf16))
    return pl.pallas_call(
        functools.partial(assemble_kernel, layout, steps, with_small),
        in_specs=[spec(pltpu.SMEM)] + [spec(pl.ANY)] * (len(flat) + len(after)),
        out_specs=[spec(pltpu.VMEM)] * len(shapes),
        out_shape=shapes,
        scratch_shapes=scratch,
        **settings(2),
    )(where, *flat, *after)


def columns_out_kernel(place_ref, group_ref, all_ref, *refs):
    ups, heads = refs[:GROUP], refs[GROUP : 2 * GROUP]
    heads_out_ref, up_out_ref, small_ref, own_ref = refs[2 * GROUP :]
    rows, hidden_part = ups[0].shape
    part = heads[0].shape[1] // 3
    for mask in range(GROUP):
        to = jnp.bitwise_xor(place_ref[0], mask)
        at = pl.multiple_of(to * hidden_part, hidden_part)
        up_out_ref[:, pl.ds(at, hidden_part)] = ups[mask][...].astype(f32)
        for k in range(3):
            at = pl.multiple_of((k * GROUP + to) * part, part)
            heads_out_ref[:, pl.ds(at, part)] = heads[mask][:, k * part : (k + 1) * part].astype(f32)
    tile = pl.ds(pl.multiple_of(place_ref[4] * 128, 128), 128)
    row = lax.broadcasted_iota(jnp.int32, (8, 128), 0)
    value = jnp.where(row < 2, all_ref[:, tile], group_ref[:, tile])
    small_ref[...] = pltpu.roll(value, lax.rem(128 - place_ref[3] * rows, 128), 1)
    own_ref[...] = group_ref[:, pl.ds(pl.multiple_of(place_ref[5] * 128, 128), 128)]


def columns_out(where, group_sums, all_sums, ups, heads):
    rows, hidden_part = ups[0].shape
    return pl.pallas_call(
        columns_out_kernel,
        in_specs=[spec(pltpu.SMEM)] + [spec(pltpu.VMEM)] * (2 * GROUP + 2),
        out_specs=[spec(pltpu.VMEM)] * 4,
        out_shape=[
            jax.ShapeDtypeStruct((rows, GROUP * heads[0].shape[1]), f32),
            jax.ShapeDtypeStruct((rows, GROUP * hidden_part), f32),
            jax.ShapeDtypeStruct((8, 128), f32),
            jax.ShapeDtypeStruct((8, 128), f32),
        ],
        **settings(4),
    )(where, group_sums, all_sums, *ups, *heads)


class Place:
    def __init__(self, sizes):
        self.ndp = sizes["dp"]
        self.no = self.ndp // GROUP
        self.nf = sizes["fsdp"]
        self.nz = self.nf // CORES
        fsdp = lax.axis_index("fsdp")
        self.dp = lax.axis_index("dp")
        self.t = self.dp % GROUP
        self.z = fsdp // CORES
        self.c = fsdp % CORES
        self.outer_groups = [[o * GROUP + t for o in range(self.no)] for t in range(GROUP)]

    def send(self, x, to):
        pairs = []
        for d in range(self.ndp):
            for z in range(self.nz):
                for c in range(CORES):
                    d2, z2, c2 = to(d, z, c)
                    pairs.append(
                        (d * self.nf + z * CORES + c, d2 * self.nf + z2 * CORES + c2)
                    )
        return lax.ppermute(x, AXES, pairs)

    def swap_t(self, x, mask):
        return self.send(x, lambda d, z, c: (d ^ mask, z, c))

    def shift_z(self, x, step=1):
        return self.send(x, lambda d, z, c: (d, (z + step) % self.nz, c))

    def swap_core(self, x):
        return self.send(x, lambda d, z, c: (d, z, CORES - 1 - c))


def later(x, *after):
    return lax.optimization_barrier((x,) + after)[0]


def add(a, b):
    return a.astype(f32) + b.astype(f32)


class RingSum:
    def __init__(self, place, where, theirs, mine):
        self.place, self.where, self.mine = place, where, mine
        self.got = place.swap_core(theirs)

    def run(self, kernel, arrays, outs, after=()):
        return call(kernel, [self.where, *arrays], outs, 6, after)[0]

    def begin(self, *after):
        kernel = functools.partial(ring_begin_kernel, self.place.nz)
        self.block = shape16(*self.mine.shape[1:])
        outs = [shape16(*self.mine.shape), self.block]
        self.chip, self.last = self.run(kernel, [self.mine, self.got], outs, after)
        self.moving = self.place.shift_z(self.last)
        self.sent = 1

    def step(self, *after):
        self.sent += 1
        kernel = functools.partial(ring_add_kernel, self.place.nz, self.sent)
        (self.last,) = self.run(kernel, [self.chip, self.moving], [self.block], after)
        self.moving = self.place.shift_z(self.last)

    def finish(self, kernel, outs, *after):
        while self.sent < self.place.nz - 1:
            self.step()
        return self.run(kernel, [self.chip, self.moving], outs, after)


class PlainSum:
    def __init__(self, place, terms):
        self.total = self.last = self.moving = plain_sum(place, terms)

    def begin(self, *after):
        pass

    step = begin


def plain_sum(place, terms):
    terms = lax.psum_scatter(terms, "dp", scatter_dimension=0, axis_index_groups=place.outer_groups)
    theirs = lax.dynamic_index_in_dim(terms, 1 - place.c, 1, keepdims=False)
    chip = lax.dynamic_index_in_dim(terms, place.c, 1, keepdims=False)
    chip = add(chip, place.swap_core(theirs)).astype(bf16)
    moving = None
    for step in range(1, place.nz + 1):
        own = lax.dynamic_index_in_dim(chip, (place.z - step) % place.nz, 0, keepdims=False)
        moving = own if moving is None else add(place.shift_z(moving), own).astype(bf16)
    return moving


def columns(place, heads_weight, up_weight, mask):
    rows, width3 = heads_weight.shape
    part = width3 // 3 // GROUP
    hidden_part = up_weight.shape[1] // GROUP
    to = place.t ^ mask
    joint = [
        lax.dynamic_slice_in_dim(heads_weight, (k * GROUP + to) * part, part, axis=1)
        for k in range(3)
    ]
    up = lax.dynamic_slice_in_dim(up_weight, to * hidden_part, hidden_part, axis=1)
    return jnp.concatenate(joint + [up], axis=1)


def spread(vector, at, count):
    n = vector.shape[0]
    row = jnp.tile(vector.astype(f32).reshape(1, n), (1, count))
    lane = lax.broadcasted_iota(jnp.int32, row.shape, 1)
    return jnp.where(lane // n == at, row, 0.0)


def small_gather(place, norm_gain, norm_bias, down_bias, up_bias, offsets, terminal):
    here = ((place.dp * place.nz) + place.z) * CORES + place.c
    count = place.ndp * place.nf
    rows = jnp.concatenate([spread(v, here, count) for v in (norm_gain, norm_bias, down_bias)])
    fsdp = (place.dp // GROUP * place.nz + place.z) * CORES + place.c
    own = spread(up_bias, fsdp, place.no * place.nf)
    lanes = rows.shape[1]
    both = jnp.concatenate([rows, jnp.pad(own, ((0, 0), (0, lanes - own.shape[1])))])
    if place.no > 1:
        both = lax.psum(both, "dp", axis_index_groups=place.outer_groups)
    shifted = [place.shift_z(both, s) for s in range(1, place.nz)]
    both = sum(shifted, both)
    both = both + place.swap_core(both)
    ends = jnp.concatenate([offsets, terminal]).astype(f32).reshape(1, -1)
    ends = jnp.pad(ends, ((0, 0), (0, lanes - ends.shape[1])))
    group = jnp.concatenate([both[:3], ends])
    others = [place.swap_t(group, m) for m in range(1, GROUP)]
    rows = sum((o[:3] for o in others), group[:3])
    windows = offsets.shape[0]
    ends = jnp.concatenate([g[3:4, : 2 * windows] for g in [group] + others])
    return rows, both[3:4, : own.shape[1]], ends


def shards(
    sizes,
    tokens,
    heads_weight,
    merge_weight,
    up_weight,
    up_bias,
    down_weight,
    down_bias,
    norm_gain,
    norm_bias,
    offsets,
    terminal,
    cotangent,
):
    place = Place(sizes)
    nz, no = place.nz, place.no
    _, length, width = tokens.shape
    half = length // 2
    head = width // HEADS
    rows = heads_weight.shape[0]
    hidden_rows = down_weight.shape[0]
    part = width // GROUP
    hidden_part = up_weight.shape[1] // GROUP
    fast = no == 1 and rows % 16 == 0 and 128 % rows == 0 and hidden_rows == 128 and part % 128 == 0
    number = place.dp * place.nf + place.z * CORES + place.c
    per = max(128 // rows, 1)
    fsdp = place.z * CORES + place.c
    where = jnp.stack([place.t, place.z, place.c, number % per, number // per, fsdp])
    where = where.astype(jnp.int32)
    own_tokens = tokens.reshape(length, width)
    own_grad = cotangent.reshape(length, width)

    if fast:
        vectors, at = 0.0, 0
        for v in (norm_gain, norm_bias, down_bias, up_bias):
            v = v.astype(f32)
            at = at if v.shape[0] < 128 else 128
            vectors += jnp.pad(v, (at, 256 - at - v.shape[0]))
            at += v.shape[0]
        *pieces, rows_block, tokens_low, tokens_high, grad_low, grad_high, _ = prepare(
            where,
            jnp.concatenate([offsets, terminal]),
            vectors.reshape(2, 128),
            heads_weight,
            up_weight,
            down_weight,
            merge_weight,
            own_tokens,
            own_grad,
        )
        joint = 3 * part + 128
    else:
        pieces = [columns(place, heads_weight, up_weight, m) for m in range(GROUP)]
        rows_block = jnp.concatenate([down_weight, merge_weight])
        tokens_low, tokens_high = own_tokens[:half], own_tokens[half:]
        grad_low, grad_high = own_grad[:half], own_grad[half:]
        joint = 3 * part
    arrived = [place.swap_t(pieces[m], m) for m in range(1, GROUP)]
    pieces = [pieces[0]] + arrived

    def outer(block):
        if no == 1:
            return block
        return lax.all_gather(block, "dp", axis_index_groups=place.outer_groups, tiled=True)

    joint_blocks = [outer(jnp.concatenate([p[:, :joint] for p in pieces]))]
    up_blocks = [outer(jnp.concatenate([p[:, joint:] for p in pieces]))]
    row_blocks = [outer(rows_block)]
    row_blocks.append(place.shift_z(row_blocks[0]))
    joint_blocks.append(place.shift_z(later(joint_blocks[0], row_blocks[1])))
    one_low = place.swap_t(later(tokens_low, *arrived), 1)
    two_high = place.swap_t(later(tokens_high, *arrived), 2)
    joint_swaps = [place.swap_core(joint_blocks[0])]
    up_blocks.append(place.shift_z(later(up_blocks[0], joint_blocks[1])))
    up_swaps = [place.swap_core(up_blocks[0])]
    joint_blocks.append(place.shift_z(later(joint_blocks[1], joint_swaps[0], one_low, two_high)))
    one_high = place.swap_t(later(tokens_high, one_low, two_high), 1)
    two_low = place.swap_t(later(tokens_low, one_low, two_high), 2)
    joint_swaps.append(place.swap_core(joint_blocks[1]))
    up_blocks.append(place.shift_z(later(up_blocks[1], up_swaps[0])))
    for step in range(3, nz):
        joint_blocks.append(
            place.shift_z(later(joint_blocks[-1], joint_swaps[1], one_high, two_low))
        )
    three_low = place.swap_t(one_low, 2)
    three_high = place.swap_t(two_high, 1)
    up_swaps.append(place.swap_core(up_blocks[1]))
    for step in range(3, nz):
        up_blocks.append(place.shift_z(later(up_blocks[-1], up_swaps[1])))
    for block in joint_blocks[2:-1]:
        joint_swaps.append(place.swap_core(block))
    joint_swaps.append(place.swap_core(later(joint_blocks[-1], three_low, three_high)))
    joint_pairs = list(zip(joint_blocks, joint_swaps))
    row_swaps = [place.swap_core(row_blocks[0])]
    row_blocks.append(place.shift_z(later(row_blocks[1], joint_blocks[-1], row_swaps[0])))
    row_swaps.append(place.swap_core(row_blocks[1]))
    grad_one_low = place.swap_t(later(grad_low, three_low, three_high), 1)
    grad_two_high = place.swap_t(later(grad_high, three_low, three_high), 2)

    if fast:
        heads, small = assemble(place, where, joint_pairs, [(rows, GROUP)], True)
        ends = joint_blocks[0]
    else:
        (heads,) = assemble(place, where, joint_pairs, [(rows, GROUP)])
        small, up_shift, ends = small_gather(
            place, norm_gain, norm_bias, down_bias, up_bias, offsets, terminal
        )
        up_shift = jnp.pad(up_shift, ((0, 4), (0, width - hidden_part)))
        small = jnp.concatenate([small, up_shift])
        ends = jnp.stack([ends // 16, ends % 16], axis=-1).reshape(GROUP, 1, 4)
        ends = jnp.pad(ends, ((0, 0), (4, 11), (0, 124))).reshape(16 * GROUP, 128)
    tables = turn_tables(length, head, 128)

    def attended_window(window, tokens, *after):
        return attend(window, ends, tokens, heads, small, tables, head, after)

    saved, units = [None] * GROUP, [None] * GROUP
    saved[0], done = attended_window(0, [tokens_low, tokens_high])
    saved[1], done = attended_window(1, [one_low, one_high], done, grad_one_low, grad_two_high)
    for block in up_blocks[2:]:
        up_swaps.append(place.swap_core(later(block, done)))
    grad_one_high = place.swap_t(later(grad_high, grad_one_low, grad_two_high, done), 1)
    grad_two_low = place.swap_t(later(grad_low, grad_one_low, grad_two_high, done), 2)
    saved[2], done = attended_window(2, [two_low, two_high], done)
    up_pairs = list(zip(up_blocks, up_swaps))
    (up,) = assemble(place, where, up_pairs, [(rows, GROUP)], after=[done, row_blocks[2]])
    for step in range(3, nz):
        row_blocks.append(place.shift_z(later(row_blocks[-1], row_swaps[1], up)))
    row_swaps.append(place.swap_core(later(row_blocks[2], up)))
    for window in range(3):
        units[window], done = hidden_units(saved[window][0], up, small, [done])
    saved[3], done = attended_window(
        3, [three_low, three_high], done, grad_one_high, grad_two_low, row_swaps[2]
    )
    grad_three_low = place.swap_t(later(grad_one_low, grad_one_high, grad_two_low), 2)
    grad_three_high = place.swap_t(later(grad_two_high, grad_one_high, grad_two_low), 1)
    for block in row_blocks[3:]:
        row_swaps.append(place.swap_core(later(block, done)))
    units[3], done = hidden_units(saved[3][0], up, small, [done])
    row_pairs = list(zip(row_blocks, row_swaps))
    down, merge = assemble(place, where, row_pairs, [(hidden_rows, 1), (rows, 1)], after=[done])
    acts, normed, attended, qkv, lse = zip(*saved)
    activated, slope = zip(*units)

    grads = [
        (grad_low, grad_high),
        (grad_one_low, grad_one_high),
        (grad_two_low, grad_two_high),
        (grad_three_low, grad_three_high),
    ]

    def out_of(window, *after):
        return out_terms(activated[window], attended[window], down, merge, after)

    def by_place(terms):
        terms = terms.reshape(no, GROUP, nz, CORES, rows, terms.shape[1])
        return terms.transpose(0, 2, 3, 1, 4, 5)

    def column_sum(grads, *after):
        if fast:
            (theirs, mine), done = column_grads(where, nz, rows, acts, grads, after)
            return RingSum(place, where, theirs, mine), done
        left, right = jnp.concatenate(acts), jnp.concatenate(grads)
        return PlainSum(place, by_place(dot(left, right, ((0,), (0,))).astype(bf16))), after[0]

    def row_sum_of(*after):
        flat = [h for pair in grads for h in pair]
        if fast:
            (theirs, mine), done = row_grads(where, nz, rows, activated, attended, flat, after)
            return RingSum(place, where, theirs, mine), done
        grad = jnp.concatenate(flat)
        down_terms = dot(jnp.concatenate(activated), grad, ((0,), (0,))).astype(bf16)
        merge_terms = dot(jnp.concatenate(attended), grad, ((0,), (0,))).astype(bf16)
        down_terms = down_terms.reshape(no, nz, CORES, hidden_rows, width)
        merge_terms = merge_terms.reshape(no, nz, CORES, rows, width)
        return PlainSum(place, jnp.concatenate([down_terms, merge_terms], axis=3)), after[0]

    outs = [None] * GROUP
    outs[3], done = out_of(3, done)
    out_low = place.swap_t(outs[3][0], 2)
    out_high = place.swap_t(outs[3][1], 1)
    hidden_grad, attended_grad = [None] * GROUP, [None] * GROUP
    joined_sums = [None] * GROUP
    for w in range(GROUP):
        (hidden_grad[w], attended_grad[w], joined_sums[w]), done = joined_grad(
            grads[w], down, merge, slope[w], [done]
        )
    row_sum, done = row_sum_of(done)
    outs[1], done = out_of(1, done)
    outs[2], done = out_of(2, done)
    out_one = [None, place.swap_t(outs[1][1], 1)]
    out_two = [place.swap_t(outs[2][0], 2), None]
    (one_low, two_high), done = add_pairs(outs[1][0], out_low, outs[2][1], out_high, after=[done])
    out_one[0] = place.swap_t(one_low, 1)
    out_two[1] = place.swap_t(two_high, 2)
    row_sum.begin(done)

    def back(window, *after):
        (mixed,), done = attend_back(
            window, ends, qkv[window], attended_grad[window], lse[window], tables, head, after
        )
        return mixed, done

    def acts_of(w, *after):
        return acts_grad(heads, up, mixed_grad[w], hidden_grad[w], normed[w], after)

    mixed_grad, terms, acts_sums = [None] * GROUP, [None] * GROUP, [None] * GROUP
    up_sum, done = column_sum(hidden_grad, done, row_sum.last)
    mixed_grad[3], done = back(3, done)
    up_sum.begin(done)
    terms[3], acts_sums[3], done = acts_of(3, done, up_sum.last)
    low = place.swap_t(terms[3][0], 2)
    high = place.swap_t(terms[3][1], 1)
    mixed_grad[1], done = back(1, done, row_sum.moving)
    row_sum.step(done)
    terms[1], acts_sums[1], done = acts_of(1, done, row_sum.last)
    one = [None, place.swap_t(terms[1][1], 1)]
    mixed_grad[2], done = back(2, done, up_sum.moving)
    up_sum.step(done)
    terms[2], acts_sums[2], done = acts_of(2, done, up_sum.last)
    two = [place.swap_t(terms[2][0], 2), None]
    mixed_grad[0], done = back(0, done, row_sum.moving, *out_one, *out_two)
    row_sum.step(done)
    heads_sum, done = column_sum(mixed_grad, done, up_sum.moving, row_sum.last)
    (one_low, two_high), done = add_pairs(terms[1][0], low, terms[2][1], high, after=[done])
    one[0] = place.swap_t(one_low, 1)
    two[1] = place.swap_t(two_high, 2)
    up_sum.step(done)
    terms[0], acts_sums[0], done = acts_of(0, done, up_sum.last)
    heads_sum.begin(done)
    outs[0], done = out_of(0, done, heads_sum.last, row_sum.moving)
    block_output = finish(
        finish_out_kernel,
        [tokens_low, tokens_high, small],
        [outs[0], out_one, out_two],
        [done],
    )

    (group_sums,), _ = call(
        small_sums_kernel,
        [*acts_sums, *joined_sums],
        [jax.ShapeDtypeStruct((8, width), f32)],
        2,
    )
    group_sums = group_sums + place.swap_core(group_sums)
    if no > 1:
        group_sums = lax.psum(group_sums, "dp", axis_index_groups=place.outer_groups)
    shifted = [place.shift_z(group_sums, s) for s in range(1, nz)]
    group_sums = sum(shifted, group_sums)
    all_sums = sum((place.swap_t(group_sums, m) for m in range(1, GROUP)), group_sums)

    def exchanged(blocks):
        return [blocks[0]] + [place.swap_t(blocks[m], m) for m in range(1, GROUP)]

    def finish_acts(*after):
        return finish(
            finish_grad_kernel,
            [tokens_low, tokens_high, grad_low, grad_high, small],
            [terms[0], one, two],
            after,
        )

    if fast:
        blocks = [shape16(rows, hidden_part)] * GROUP
        up_arrived = exchanged(up_sum.finish(ring_columns_kernel, blocks))
        heads_sum.step(block_output)
        grad_tokens = finish_acts()
        heads_sum.step(grad_tokens, *up_arrived[1:])
        blocks = [shape16(rows, 3 * part)] * GROUP
        heads_arrived = exchanged(heads_sum.finish(ring_columns_kernel, blocks))
        both = [jax.ShapeDtypeStruct((n, width), f32) for n in (hidden_rows, rows)]
        grad_down, grad_merge = row_sum.finish(ring_rows_kernel, both)
        grad_heads, grad_up, narrow, own = columns_out(
            where, group_sums, all_sums, up_arrived, heads_arrived
        )
        grad_gain, grad_bias, grad_down_bias = (narrow[k, :rows] for k in range(3))
        grad_up_bias = own[3, :hidden_rows]
    else:
        grad_tokens = finish_acts()

        def by_t(summed):
            blocks = [
                lax.dynamic_index_in_dim(summed, place.t ^ m, 0, keepdims=False)
                for m in range(GROUP)
            ]
            arrived = exchanged(blocks)
            return [lax.select_n(t ^ place.t, *arrived).astype(f32) for t in range(GROUP)]

        row_total = row_sum.total.astype(f32)
        grad_down, grad_merge = row_total[:hidden_rows], row_total[hidden_rows:]
        heads_by_t = by_t(heads_sum.total)
        grad_heads = jnp.concatenate(
            [h[:, k * part : (k + 1) * part] for k in range(3) for h in heads_by_t], axis=1
        )
        grad_up = jnp.concatenate(by_t(up_sum.total), axis=1)
        at = number * rows
        grad_gain, grad_bias = (
            lax.dynamic_slice_in_dim(all_sums[k], at, rows) for k in range(2)
        )
        grad_down_bias = lax.dynamic_slice_in_dim(group_sums[2], at, rows)
        at = (place.dp // GROUP * place.nf + fsdp) * hidden_rows
        grad_up_bias = lax.dynamic_slice_in_dim(group_sums[3], at, hidden_rows)
    return (
        block_output.reshape(tokens.shape),
        grad_tokens.reshape(tokens.shape),
        grad_heads,
        grad_merge,
        grad_up,
        grad_up_bias,
        grad_down,
        grad_down_bias,
        grad_gain,
        grad_bias,
    )


def solution(mesh):
    whole = P(AXES)
    return jax.shard_map(
        functools.partial(shards, dict(mesh.shape)),
        mesh=mesh,
        in_specs=(whole,) * 12,
        out_specs=(whole,) * 10,
        check_vma=False,
    )
```

time: 320 us -> 242 us (0.76)
  waiting for transfers between devices: 140 us -> 73.7 us
  Pallas kernels: 32.2 us -> 97.6 us
  matrix products: 46 us -> 0 us
  other arithmetic: 30.7 us -> 0.93 us
  starting transfers between devices: 42.3 us -> 60.6 us
  local copies, waits for them, and re-layouts: 20.5 us -> 3.48 us
    ppermute x51 -> x73, waiting for transfers between devices: 140 us -> 73.7 us  [send(): return lax.ppermute(x, AXES, pairs)]
    pallas_call x4 -> x49, Pallas kernels: 32.2 us -> 97.6 us  [the longest x44 84.8 us: call(): pl.pallas_call(body, in_specs=[spec(pltpu.SMEM if x.dtype == jnp.int32 el...]
    dot_general x6 -> x0, matrix products: 46 us -> none  [dot(): return lax.dot_general(a, b, (dims, ((), ())), preferred_element_type=f32)]
    ppermute x51 -> x73, starting transfers between devices: 42.3 us -> 60.6 us  [send(): return lax.ppermute(x, AXES, pairs)]
    reduce_sum x12 -> x0, other arithmetic: 14.4 us -> none  [the longest x1 5.91 us: shards(): grad_up_bias = jnp.sum(hidden_grad.astype(f32), axis=0)]
    convert_element_type x18 -> x0, other arithmetic: 7.84 us -> none  [the longest x1 4.24 us: shards(): activated = gelu_tanh(hidden).astype(bf16)]
    unnamed x60 -> x8, local copies, waits for them, and re-layouts: 8.35 us -> 2.32 us
    slice x21 -> x8, local copies, waits for them, and re-layouts: 5.96 us -> 0.05 us  [the longest x4 0.02 us: shards(): up_blocks = [outer(jnp.concatenate([p[:, joint:] for p in pieces]))]]
  transfers between devices with their start and end apart: 51 -> 73, of which waited for: 19 -> 30; matrix products, arithmetic and copies ran while one was open for 27% -> 0% of each run, Pallas kernels for 10% -> 32%
where the time goes in v2:
time: 242 us; the launch traced here: 239 us
  Pallas kernels  97.6 us (40%)
  waiting for transfers between devices  73.7 us (30%)
  starting transfers between devices  60.6 us (25%)
  local copies, waits for them, and re-layouts  3.48 us (1%)
  between operations  2.89 us (1%)
    pallas_call x44, Pallas kernels, call(): pl.pallas_call(body, in_specs=[spec(pltpu.SMEM if x.dtype == jnp.int32 el...  84.8 us
    ppermute x73, waiting for transfers between devices, send(): return lax.ppermute(x, AXES, pairs)  73.7 us
    ppermute x73, starting transfers between devices, send(): return lax.ppermute(x, AXES, pairs)  60.6 us
    pallas_call x3, Pallas kernels, assemble(): pl.pallas_call(functools.partial(assemble_kernel, layout, steps, with_sma...  8.21 us
  transfers between devices with their start and end apart: 73, of which 30 were waited for; matrix products, arithmetic and copies ran while one was open for 0% of the time, Pallas kernels for 32%

profile of v2, /device:TPU:0, one launch (start us, length us, event | category | flops | bytes accessed | tf_op | source)
XLA Modules:
  0.0 239.2 jit_solution(17793436997622898111)
XLA Ops:
  2.9 3.1 %shard_map.213 = (bf16[32,1920]{1,0:T(8,128)(2,1)S(1)}, bf16[32,1920]{1,0:T(8,128)(2,1)S(1)}, bf16[32,1920]{1,0:T(8,128)(2,1)S(1)}, bf16[32,1920]{1,0:T(8,128)(2...) custom-call(s32[6]{0:T(128)S(1)} %stack.27.place_ref.refs_0_, ...), custom_call_target="tpu_custom_call" | custom-call | flops 1 | bytes 1 | tf_op jit(solution)/shard_map/pallas_call | solution.py:510
  6.1 3.1 %collective-permute-start.4 = (bf16[160,1024]{1,0:T(8,128)(2,1)S(1)}, bf16[160,1024]{1,0:T(8,128)(2,1)S(1)}, u32[]{:S(2)}, u32[]{:S(2)}) collective-permute-start(bf16[160,1024]{1,0:T(8,128)(2,1)S(1)} %get-tuple-element.184.refs_0_), channel_id=1, source_target_pairs={{0,2},{1,3},{2,4},{3,5},{4,6},{5,7},{6,0},{7,1},{8,10},{9,11},{10,... | collective-permute-start | bytes 983048 | tf_op jit(solution)/shard_map/ppermute | solution.py:664
  14.4 3.8 %collective-permute-done.1 = bf16[32,1920]{1,0:T(8,128)(2,1)S(1)} collective-permute-done((bf16[32,1920]{1,0:T(8,128)(2,1)S(1)}, bf16[32,1920]{1,0:T(8,128)(2,1)S(1)}, u32[]{:S(2)}, u32[]{:S(2)}) %collective-permute-start.1) | collective-permute-done | bytes 122912 | tf_op jit(solution)/shard_map/ppermute | solution.py:664
  22.3 5.6 %collective-permute-done.5.refs_2_ = bf16[128,896]{1,0:T(8,128)(2,1)S(1)} collective-permute-done((bf16[128,896]{1,0:T(8,128)(2,1)S(1)}, bf16[128,896]{1,0:T(8,128)(2,1)S(1)}, u32[]{:S(2)}, u32[]{:S(2)}) %collective-permute-start.5) | collective-permute-done | bytes 229408 | tf_op jit(solution)/shard_map/ppermute | solution.py:664
  44.9 5.9 %collective-permute-done.14.refs_5_ = bf16[208,1024]{1,0:T(8,128)(2,1)S(1)} collective-permute-done((bf16[208,1024]{1,0:T(8,128)(2,1)S(1)}, bf16[208,1024]{1,0:T(8,128)(2,1)S(1)}, u32[]{:S(2)}, u32[]{:S(2)}) %collective-permute-start.14) | collective-permute-done | bytes 426016 | tf_op jit(solution)/shard_map/ppermute | solution.py:664
  60.3 3.4 %shard_map.215 = (bf16[416,1024]{1,0:T(8,128)(2,1)S(1)}, bf16[416,1024]{1,0:T(8,128)(2,1)S(1)}, bf16[416,256]{1,0:T(8,128)(2,1)S(1)}, bf16[416,768]{1,0:T(8,128)...) custom-call(bf16[128,896]{1,0:T(8,128)(2,1)S(1)} %pad_maximum_fusion.1.refs_0_, ...), custom_call_target="tpu_custom_call" | custom-call | flops 1 | bytes 1 | tf_op jit(solution)/shard_map/pallas_call | solution.py:87
  65.2 3.4 %shard_map.216 = (bf16[416,1024]{1,0:T(8,128)(2,1)S(1)}, bf16[416,1024]{1,0:T(8,128)(2,1)S(1)}, bf16[416,256]{1,0:T(8,128)(2,1)S(1)}, bf16[416,768]{1,0:T(8,128)...) custom-call(bf16[128,896]{1,0:T(8,128)(2,1)S(1)} %pad_maximum_fusion.1.refs_0_, ...), custom_call_target="tpu_custom_call" | custom-call | flops 1 | bytes 1 | tf_op jit(solution)/shard_map/pallas_call | solution.py:87
  69.7 4.4 %collective-permute-done.19.refs_9_.refs_4_ = bf16[160,1024]{1,0:T(8,128)(2,1)S(1)} collective-permute-done((bf16[160,1024]{1,0:T(8,128)(2,1)S(1)}, bf16[160,1024]{1,0:T(8,128)(2,1)S(1)}, u32[]{:S(2)}, u32[]{:S(2)}) %collective-permute-start.19) | collective-permute-done | bytes 327712 | tf_op jit(solution)/shard_map/ppermute | solution.py:664
  74.2 3.4 %shard_map.217 = (bf16[416,1024]{1,0:T(8,128)(2,1)S(1)}, bf16[416,1024]{1,0:T(8,128)(2,1)S(1)}, bf16[416,256]{1,0:T(8,128)(2,1)S(1)}, bf16[416,768]{1,0:T(8,128)...) custom-call(bf16[128,896]{1,0:T(8,128)(2,1)S(1)} %pad_maximum_fusion.1.refs_0_, ...), custom_call_target="tpu_custom_call" | custom-call | flops 1 | bytes 1 | tf_op jit(solution)/shard_map/pallas_call | solution.py:87
  77.7 4.1 %shard_map.218.refs_0_.refs_1_ = bf16[1024,1024]{1,0:T(8,128)(2,1)S(1)} custom-call(s32[6]{0:T(128)S(1)} %stack.27.place_ref.refs_0_, bf16[128,1024]{1,0:T(8,128)(2,1)S(1)} %pad_maximum_fusion.refs_0_, bf16[128,1024]{1,0:T(8,128)(2,1)S(1)} %collective-permute-done.20.refs_1_, bf16[128,1024]{1,0:T(8,128)(2,1)S(1)} %collective-permute-done.21.refs_2_, ...), custom_call_target="tpu_custom_call" | custom-call | flops 1 | bytes 1 | tf_op jit(solution)/shard_map/pallas_call | solution.py:597
  82.2 3.3 %collective-permute-done.32.refs_9_.refs_3_.refs_13_ = bf16[208,1024]{1,0:T(8,128)(2,1)S(1)} collective-permute-done((bf16[208,1024]{1,0:T(8,128)(2,1)S(1)}, bf16[208,1024]{1,0:T(8,128)(2,1)S(1)}, u32[]{:S(2)}, u32[]{:S(2)}) %collective-permute-start.32) | collective-permute-done | bytes 426016 | tf_op jit(solution)/shard_map/ppermute | solution.py:664
  92.6 3.4 %shard_map.222 = (bf16[416,1024]{1,0:T(8,128)(2,1)S(1)}, bf16[416,1024]{1,0:T(8,128)(2,1)S(1)}, bf16[416,256]{1,0:T(8,128)(2,1)S(1)}, bf16[416,768]{1,0:T(8,128)...) custom-call(bf16[128,896]{1,0:T(8,128)(2,1)S(1)} %pad_maximum_fusion.1.refs_0_, ...), custom_call_target="tpu_custom_call" | custom-call | flops 1 | bytes 1 | tf_op jit(solution)/shard_map/pallas_call | solution.py:87
  106.9 5.5 %shard_map.230 = (bf16[4,160,1024]{2,1,0:T(8,128)(2,1)S(1)}, bf16[4,160,1024]{2,1,0:T(8,128)(2,1)S(1)}, f32[8,128]{1,0:T(8,128)S(1)}) custom-call(s32[6]{0:T(128)S(1)} %stack.27.place_ref.refs_0_, bf16[416,1024]{1,0:T(8,128)(2,1)S(1)} %get-tuple-element.224.refs_1_.refs_2_, bf16[416,1024]{1,0:T(8,128)(2,1)S(1)} %get-tuple-element.254.refs_2_, ...), custom_call_target="tpu_custom_call" | custom-call | flops 1 | bytes 1 | tf_op jit(solution)/shard_map/pallas_call | solution.py:87
  118.0 6.7 %collective-permute-done.36.refs_1_ = bf16[208,1024]{1,0:T(8,128)(2,1)S(1)} collective-permute-done((bf16[208,1024]{1,0:T(8,128)(2,1)S(1)}, bf16[208,1024]{1,0:T(8,128)(2,1)S(1)}, u32[]{:S(2)}, u32[]{:S(2)}) %collective-permute-start.36) | collective-permute-done | bytes 426016 | tf_op jit(solution)/shard_map/ppermute | solution.py:664
  127.1 4.7 %shard_map.235 = (bf16[4,128,1024]{2,1,0:T(8,128)(2,1)S(1)}, bf16[4,128,1024]{2,1,0:T(8,128)(2,1)S(1)}, f32[8,128]{1,0:T(8,128)S(1)}) custom-call(s32[6]{0:T(128)S(1)} %stack.27.place_ref.refs_0_, bf16[416,1024]{1,0:T(8,128)(2,1)S(1)} %get-tuple-element.212.refs_2_.refs_1_, bf16[416,1024]{1,0:T(8,128)(2,1)S(1)} %get-tuple-element.211.refs_2_, ...), custom_call_target="tpu_custom_call" | custom-call | flops 1 | bytes 1 | tf_op jit(solution)/shard_map/pallas_call | solution.py:87
  132.9 3.3 %shard_map.236 = (bf16[416,768]{1,0:T(8,128)(2,1)S(1)}, f32[8,128]{1,0:T(8,128)S(1)}) custom-call(bf16[128,896]{1,0:T(8,128)(2,1)S(1)} %pad_maximum_fusion.1.refs_0_, f32[416,128]{1,0:T(8,128)S(1)} %copy-done.1, f32[416,128]{1,0:T(8,128)S(1)} %copy-done, bf16[416,768]{1,0:T(8,128)(2,1)S(1)} %get-tuple-element.243.refs_3_, ...), custom_call_target="tpu_custom_call" | custom-call | flops 1 | bytes 1 | tf_op jit(solution)/shard_map/pallas_call | solution.py:87
  139.4 4.9 %collective-permute-done.40.refs_7_.refs_2_ = bf16[160,1024]{1,0:T(8,128)(2,1)S(1)} collective-permute-done((bf16[160,1024]{1,0:T(8,128)(2,1)S(1)}, bf16[160,1024]{1,0:T(8,128)(2,1)S(1)}, u32[]{:S(2)}, u32[]{:S(2)}) %collective-permute-start.40) | collective-permute-done | bytes 327712 | tf_op jit(solution)/shard_map/ppermute | solution.py:664
  146.9 3.3 %shard_map.239 = (bf16[416,768]{1,0:T(8,128)(2,1)S(1)}, f32[8,128]{1,0:T(8,128)S(1)}) custom-call(bf16[128,896]{1,0:T(8,128)(2,1)S(1)} %pad_maximum_fusion.1.refs_0_, f32[416,128]{1,0:T(8,128)S(1)} %copy-done.1, f32[416,128]{1,0:T(8,128)S(1)} %copy-done, bf16[416,768]{1,0:T(8,128)(2,1)S(1)} %get-tuple-element.240.refs_3_, ...), custom_call_target="tpu_custom_call" | custom-call | flops 1 | bytes 1 | tf_op jit(solution)/shard_map/pallas_call | solution.py:87
  153.4 3.3 %shard_map.242 = (bf16[416,768]{1,0:T(8,128)(2,1)S(1)}, f32[8,128]{1,0:T(8,128)S(1)}) custom-call(bf16[128,896]{1,0:T(8,128)(2,1)S(1)} %pad_maximum_fusion.1.refs_0_, f32[416,128]{1,0:T(8,128)S(1)} %copy-done.1, f32[416,128]{1,0:T(8,128)S(1)} %copy-done, bf16[416,768]{1,0:T(8,128)(2,1)S(1)} %get-tuple-element.233.refs_3_, ...), custom_call_target="tpu_custom_call" | custom-call | flops 1 | bytes 1 | tf_op jit(solution)/shard_map/pallas_call | solution.py:87
  162.6 3.3 %shard_map.245 = (bf16[416,768]{1,0:T(8,128)(2,1)S(1)}, f32[8,128]{1,0:T(8,128)S(1)}) custom-call(bf16[128,896]{1,0:T(8,128)(2,1)S(1)} %pad_maximum_fusion.1.refs_0_, f32[416,128]{1,0:T(8,128)S(1)} %copy-done.1, f32[416,128]{1,0:T(8,128)S(1)} %copy-done, bf16[416,768]{1,0:T(8,128)(2,1)S(1)} %get-tuple-element.226.refs_3_, ...), custom_call_target="tpu_custom_call" | custom-call | flops 1 | bytes 1 | tf_op jit(solution)/shard_map/pallas_call | solution.py:87
  167.5 3.7 %shard_map.247 = (bf16[4,128,768]{2,1,0:T(8,128)(2,1)S(1)}, bf16[4,128,768]{2,1,0:T(8,128)(2,1)S(1)}, f32[8,128]{1,0:T(8,128)S(1)}) custom-call(s32[6]{0:T(128)S(1)} %stack.27.place_ref.refs_0_, bf16[416,1024]{1,0:T(8,128)(2,1)S(1)} %get-tuple-element.212.refs_2_.refs_1_, bf16[416,1024]{1,0:T(8,128)(2,1)S(1)} %get-tuple-element.211.refs_2_, ...), custom_call_target="tpu_custom_call" | custom-call | flops 1 | bytes 1 | tf_op jit(solution)/shard_map/pallas_call | solution.py:87
  174.1 9.4 %collective-permute-done.47.refs_1_ = bf16[208,1024]{1,0:T(8,128)(2,1)S(1)} collective-permute-done((bf16[208,1024]{1,0:T(8,128)(2,1)S(1)}, bf16[208,1024]{1,0:T(8,128)(2,1)S(1)}, u32[]{:S(2)}, u32[]{:S(2)}) %collective-permute-start.47) | collective-permute-done | bytes 426016 | tf_op jit(solution)/shard_map/ppermute | solution.py:664
  192.8 3.9 %collective-permute-done.67.refs_2_ = bf16[128,768]{1,0:T(8,128)(2,1)S(1)} collective-permute-done((bf16[128,768]{1,0:T(8,128)(2,1)S(1)}, bf16[128,768]{1,0:T(8,128)(2,1)S(1)}, u32[]{:S(2)}, u32[]{:S(2)}) %collective-permute-start.67) | collective-permute-done | bytes 196640 | tf_op jit(solution)/shard_map/ppermute | solution.py:664
  220.6 2.8 %collective-permute-start.69 = (bf16[128,768]{1,0:T(8,128)(2,1)S(1)}, bf16[128,768]{1,0:T(8,128)(2,1)S(1)}, u32[]{:S(2)}, u32[]{:S(2)}) collective-permute-start(bf16[128,768]{1,0:T(8,128)(2,1)S(1)} %get-tuple-element.335), channel_id=1, source_target_pairs={{0,2},{1,3},{2,4},{3,5},{4,6},{5,7},{6,0},{7,1},{8,10},{9,11},{10,... | collective-permute-start | bytes 589832 | tf_op jit(solution)/shard_map/ppermute | solution.py:664
  (197 shorter events, 134.3 us)
Async XLA Ops:
  6.1 13.9 %collective-permute-start.4 = (bf16[160,1024]{1,0:T(8,128)(2,1)S(1)}, bf16[160,1024]{1,0:T(8,128)(2,1)S(1)}, u32[]{:S(2)}, u32[]{:S(2)}) collective-permute-start(bf16[160,1024]{1,0:T(8,128)(2,1)S(1)} %get-tuple-element.184.refs_0_), channel_id=1, source_target_pairs={{0,2},{1,3},{2,4},{3,5},{4,6},{5,7},{6,0},{7,1},{8,10},{9,11},{10,... | collective-permute-start | bytes 983048 | tf_op jit(solution)/shard_map/ppermute | solution.py:664
  29.4 12.8 %collective-permute-start.11 = (bf16[208,1024]{1,0:T(8,128)(2,1)S(1)}, bf16[208,1024]{1,0:T(8,128)(2,1)S(1)}, u32[]{:S(2)}, u32[]{:S(2)}) collective-permute-start(bf16[208,1024]{1,0:T(8,128)(2,1)S(1)} %get-tuple-element.189.refs_6_.refs_1_), channel_id=1, source_target_pairs={{0,8},{1,9},{2,10},{3,11},{4,12},{5,13},{6,14},{7,15},{8,0},{9,1},... | collective-permute-start | bytes 1277960 | tf_op jit(solution)/shard_map/ppermute | solution.py:664
  29.9 12.7 %collective-permute-start.12 = (bf16[208,1024]{1,0:T(8,128)(2,1)S(1)}, bf16[208,1024]{1,0:T(8,128)(2,1)S(1)}, u32[]{:S(2)}, u32[]{:S(2)}) collective-permute-start(bf16[208,1024]{1,0:T(8,128)(2,1)S(1)} %get-tuple-element.190.refs_5_.refs_0_), channel_id=1, source_target_pairs={{0,16},{1,17},{2,18},{3,19},{4,20},{5,21},{6,22},{7,23},{8,24},{9,... | collective-permute-start | bytes 1277960 | tf_op jit(solution)/shard_map/ppermute | solution.py:664
  30.4 20.4 %collective-permute-start.14 = (bf16[208,1024]{1,0:T(8,128)(2,1)S(1)}, bf16[208,1024]{1,0:T(8,128)(2,1)S(1)}, u32[]{:S(2)}, u32[]{:S(2)}) collective-permute-start(bf16[208,1024]{1,0:T(8,128)(2,1)S(1)} %collective-permute-done.7.refs_5_), channel_id=1, source_target_pairs={{0,16},{1,17},{2,18},{3,19},{4,20},{5,21},{6,22},{7,23},{8,24},{9,... | collective-permute-start | bytes 1277960 | tf_op jit(solution)/shard_map/ppermute | solution.py:664
  36.2 14.6 %collective-permute-start.15 = (bf16[208,1024]{1,0:T(8,128)(2,1)S(1)}, bf16[208,1024]{1,0:T(8,128)(2,1)S(1)}, u32[]{:S(2)}, u32[]{:S(2)}) collective-permute-start(bf16[208,1024]{1,0:T(8,128)(2,1)S(1)} %collective-permute-done.8.refs_6_), channel_id=1, source_target_pairs={{0,8},{1,9},{2,10},{3,11},{4,12},{5,13},{6,14},{7,15},{8,0},{9,1},... | collective-permute-start | bytes 1277960 | tf_op jit(solution)/shard_map/ppermute | solution.py:664
  56.7 17.5 %collective-permute-start.19 = (bf16[160,1024]{1,0:T(8,128)(2,1)S(1)}, bf16[160,1024]{1,0:T(8,128)(2,1)S(1)}, u32[]{:S(2)}, u32[]{:S(2)}) collective-permute-start(bf16[160,1024]{1,0:T(8,128)(2,1)S(1)} %collective-permute-done.4.refs_2_), channel_id=1, source_target_pairs={{0,2},{1,3},{2,4},{3,5},{4,6},{5,7},{6,0},{7,1},{8,10},{9,11},{10,... | collective-permute-start | bytes 983048 | tf_op jit(solution)/shard_map/ppermute | solution.py:664
  58.1 23.8 %collective-permute-start.18 = (bf16[160,1024]{1,0:T(8,128)(2,1)S(1)}, bf16[160,1024]{1,0:T(8,128)(2,1)S(1)}, u32[]{:S(2)}, u32[]{:S(2)}) collective-permute-start(bf16[160,1024]{1,0:T(8,128)(2,1)S(1)} %collective-permute-done.4.refs_2_), channel_id=1, source_target_pairs={{0,1},{1,0},{2,3},{3,2},{4,5},{5,4},{6,7},{7,6},{8,9},{9,8},{10,11... | collective-permute-start | bytes 983048 | tf_op jit(solution)/shard_map/ppermute | solution.py:664
  69.2 13.0 %collective-permute-start.31 = (bf16[208,1024]{1,0:T(8,128)(2,1)S(1)}, bf16[208,1024]{1,0:T(8,128)(2,1)S(1)}, u32[]{:S(2)}, u32[]{:S(2)}) collective-permute-start(bf16[208,1024]{1,0:T(8,128)(2,1)S(1)} %get-tuple-element.216.refs_4_.refs_10_.refs_3_), channel_id=1, source_target_pairs={{0,8},{1,9},{2,10},{3,11},{4,12},{5,13},{6,14},{7,15},{8,0},{9,1},... | collective-permute-start | bytes 1277960 | tf_op jit(solution)/shard_map/ppermute | solution.py:664
  81.9 14.2 %collective-permute-start.30 = (bf16[160,1024]{1,0:T(8,128)(2,1)S(1)}, bf16[160,1024]{1,0:T(8,128)(2,1)S(1)}, u32[]{:S(2)}, u32[]{:S(2)}) collective-permute-start(bf16[160,1024]{1,0:T(8,128)(2,1)S(1)} %collective-permute-done.19.refs_9_.refs_4_), channel_id=1, source_target_pairs={{0,2},{1,3},{2,4},{3,5},{4,6},{5,7},{6,0},{7,1},{8,10},{9,11},{10,... | collective-permute-start | bytes 983048 | tf_op jit(solution)/shard_map/ppermute | solution.py:664
  85.5 19.9 %collective-permute-start.34 = (bf16[208,1024]{1,0:T(8,128)(2,1)S(1)}, bf16[208,1024]{1,0:T(8,128)(2,1)S(1)}, u32[]{:S(2)}, u32[]{:S(2)}) collective-permute-start(bf16[208,1024]{1,0:T(8,128)(2,1)S(1)} %collective-permute-done.24.refs_8_.refs_3_.refs_11_), channel_id=1, source_target_pairs={{0,16},{1,17},{2,18},{3,19},{4,20},{5,21},{6,22},{7,23},{8,24},{9,... | collective-permute-start | bytes 1277960 | tf_op jit(solution)/shard_map/ppermute | solution.py:664
  85.8 19.7 %collective-permute-start.35 = (bf16[208,1024]{1,0:T(8,128)(2,1)S(1)}, bf16[208,1024]{1,0:T(8,128)(2,1)S(1)}, u32[]{:S(2)}, u32[]{:S(2)}) collective-permute-start(bf16[208,1024]{1,0:T(8,128)(2,1)S(1)} %collective-permute-done.25.refs_9_.refs_4_.refs_14_), channel_id=1, source_target_pairs={{0,8},{1,9},{2,10},{3,11},{4,12},{5,13},{6,14},{7,15},{8,0},{9,1},... | collective-permute-start | bytes 1277960 | tf_op jit(solution)/shard_map/ppermute | solution.py:664
  112.4 13.5 %collective-permute-start.38 = (bf16[4,160,1024]{2,1,0:T(8,128)(2,1)S(1)}, bf16[4,160,1024]{2,1,0:T(8,128)(2,1)S(1)}, u32[]{:S(2)}, u32[]{:S(2)}) collective-permute-start(bf16[4,160,1024]{2,1,0:T(8,128)(2,1)S(1)} %get-tuple-element.268), channel_id=1, source_target_pairs={{0,1},{1,0},{2,3},{3,2},{4,5},{5,4},{6,7},{7,6},{8,9},{9,8},{10,11... | collective-permute-start | bytes 3932168 | tf_op jit(solution)/shard_map/ppermute | solution.py:664
  132.0 25.8 %collective-permute-start.45 = (bf16[208,1024]{1,0:T(8,128)(2,1)S(1)}, bf16[208,1024]{1,0:T(8,128)(2,1)S(1)}, u32[]{:S(2)}, u32[]{:S(2)}) collective-permute-start(bf16[208,1024]{1,0:T(8,128)(2,1)S(1)} %get-tuple-element.292), channel_id=1, source_target_pairs={{0,16},{1,17},{2,18},{3,19},{4,20},{5,21},{6,22},{7,23},{8,24},{9,... | collective-permute-start | bytes 1277960 | tf_op jit(solution)/shard_map/ppermute | solution.py:664
  137.4 14.0 %collective-permute-start.41 = (bf16[128,1024]{1,0:T(8,128)(2,1)S(1)}, bf16[128,1024]{1,0:T(8,128)(2,1)S(1)}, u32[]{:S(2)}, u32[]{:S(2)}) collective-permute-start(bf16[128,1024]{1,0:T(8,128)(2,1)S(1)} %get-tuple-element.276.refs_6_), channel_id=1, source_target_pairs={{0,2},{1,3},{2,4},{3,5},{4,6},{5,7},{6,0},{7,1},{8,10},{9,11},{10,... | collective-permute-start | bytes 786440 | tf_op jit(solution)/shard_map/ppermute | solution.py:664
  137.4 22.6 %collective-permute-start.44 = (bf16[208,1024]{1,0:T(8,128)(2,1)S(1)}, bf16[208,1024]{1,0:T(8,128)(2,1)S(1)}, u32[]{:S(2)}, u32[]{:S(2)}) collective-permute-start(bf16[208,1024]{1,0:T(8,128)(2,1)S(1)} %get-tuple-element.291), channel_id=1, source_target_pairs={{0,8},{1,9},{2,10},{3,11},{4,12},{5,13},{6,14},{7,15},{8,0},{9,1},... | collective-permute-start | bytes 1277960 | tf_op jit(solution)/shard_map/ppermute | solution.py:664
  138.2 21.8 %collective-permute-start.43 = (bf16[208,1024]{1,0:T(8,128)(2,1)S(1)}, bf16[208,1024]{1,0:T(8,128)(2,1)S(1)}, u32[]{:S(2)}, u32[]{:S(2)}) collective-permute-start(bf16[208,1024]{1,0:T(8,128)(2,1)S(1)} %get-tuple-element.290), channel_id=1, source_target_pairs={{0,8},{1,9},{2,10},{3,11},{4,12},{5,13},{6,14},{7,15},{8,0},{9,1},... | collective-permute-start | bytes 1277960 | tf_op jit(solution)/shard_map/ppermute | solution.py:664
  144.3 15.7 %collective-permute-start.46 = (bf16[208,1024]{1,0:T(8,128)(2,1)S(1)}, bf16[208,1024]{1,0:T(8,128)(2,1)S(1)}, u32[]{:S(2)}, u32[]{:S(2)}) collective-permute-start(bf16[208,1024]{1,0:T(8,128)(2,1)S(1)} %get-tuple-element.293), channel_id=1, source_target_pairs={{0,16},{1,17},{2,18},{3,19},{4,20},{5,21},{6,22},{7,23},{8,24},{9,... | collective-permute-start | bytes 1277960 | tf_op jit(solution)/shard_map/ppermute | solution.py:664
  171.2 16.4 %collective-permute-start.50 = (bf16[4,128,768]{2,1,0:T(8,128)(2,1)S(1)}, bf16[4,128,768]{2,1,0:T(8,128)(2,1)S(1)}, u32[]{:S(2)}, u32[]{:S(2)}) collective-permute-start(bf16[4,128,768]{2,1,0:T(8,128)(2,1)S(1)} %get-tuple-element.307), channel_id=1, source_target_pairs={{0,1},{1,0},{2,3},{3,2},{4,5},{5,4},{6,7},{7,6},{8,9},{9,8},{10,11... | collective-permute-start | bytes 2359304 | tf_op jit(solution)/shard_map/ppermute | solution.py:664
  173.9 17.7 %collective-permute-start.51 = (bf16[160,1024]{1,0:T(8,128)(2,1)S(1)}, bf16[160,1024]{1,0:T(8,128)(2,1)S(1)}, u32[]{:S(2)}, u32[]{:S(2)}) collective-permute-start(bf16[160,1024]{1,0:T(8,128)(2,1)S(1)} %get-tuple-element.301.refs_11_), channel_id=1, source_target_pairs={{0,2},{1,3},{2,4},{3,5},{4,6},{5,7},{6,0},{7,1},{8,10},{9,11},{10,... | collective-permute-start | bytes 983048 | tf_op jit(solution)/shard_map/ppermute | solution.py:664
  188.8 12.9 %collective-permute-start.53 = (bf16[208,1024]{1,0:T(8,128)(2,1)S(1)}, bf16[208,1024]{1,0:T(8,128)(2,1)S(1)}, u32[]{:S(2)}, u32[]{:S(2)}) collective-permute-start(bf16[208,1024]{1,0:T(8,128)(2,1)S(1)} %get-tuple-element.316), channel_id=1, source_target_pairs={{0,8},{1,9},{2,10},{3,11},{4,12},{5,13},{6,14},{7,15},{8,0},{9,1},... | collective-permute-start | bytes 1277960 | tf_op jit(solution)/shard_map/ppermute | solution.py:664
  190.0 18.2 %collective-permute-start.54 = (bf16[208,1024]{1,0:T(8,128)(2,1)S(1)}, bf16[208,1024]{1,0:T(8,128)(2,1)S(1)}, u32[]{:S(2)}, u32[]{:S(2)}) collective-permute-start(bf16[208,1024]{1,0:T(8,128)(2,1)S(1)} %get-tuple-element.317), channel_id=1, source_target_pairs={{0,16},{1,17},{2,18},{3,19},{4,20},{5,21},{6,22},{7,23},{8,24},{9,... | collective-permute-start | bytes 1277960 | tf_op jit(solution)/shard_map/ppermute | solution.py:664
  190.4 24.9 %collective-permute-start.52 = (bf16[208,1024]{1,0:T(8,128)(2,1)S(1)}, bf16[208,1024]{1,0:T(8,128)(2,1)S(1)}, u32[]{:S(2)}, u32[]{:S(2)}) collective-permute-start(bf16[208,1024]{1,0:T(8,128)(2,1)S(1)} %get-tuple-element.315), channel_id=1, source_target_pairs={{0,8},{1,9},{2,10},{3,11},{4,12},{5,13},{6,14},{7,15},{8,0},{9,1},... | collective-permute-start | bytes 1277960 | tf_op jit(solution)/shard_map/ppermute | solution.py:664
  191.6 23.7 %collective-permute-start.55 = (bf16[208,1024]{1,0:T(8,128)(2,1)S(1)}, bf16[208,1024]{1,0:T(8,128)(2,1)S(1)}, u32[]{:S(2)}, u32[]{:S(2)}) collective-permute-start(bf16[208,1024]{1,0:T(8,128)(2,1)S(1)} %get-tuple-element.318), channel_id=1, source_target_pairs={{0,16},{1,17},{2,18},{3,19},{4,20},{5,21},{6,22},{7,23},{8,24},{9,... | collective-permute-start | bytes 1277960 | tf_op jit(solution)/shard_map/ppermute | solution.py:664
  201.7 16.6 %collective-permute-start.68 = (bf16[128,768]{1,0:T(8,128)(2,1)S(1)}, bf16[128,768]{1,0:T(8,128)(2,1)S(1)}, u32[]{:S(2)}, u32[]{:S(2)}) collective-permute-start(bf16[128,768]{1,0:T(8,128)(2,1)S(1)} %get-tuple-element.334), channel_id=1, source_target_pairs={{0,2},{1,3},{2,4},{3,5},{4,6},{5,7},{6,0},{7,1},{8,10},{9,11},{10,... | collective-permute-start | bytes 589832 | tf_op jit(solution)/shard_map/ppermute | solution.py:664
  (53 other events, 479.0 us)
